TPU v7x, 32 devices: a whole 2x2x4 slice. The times are simulated.
32 devices in a mesh: seq: 8 (over z, x), hap: 4 (over y, core).
Axes of the slice: x: 2, y: 2, z: 4, core: 2. Of those that a mesh axis runs over, the one named last changes fastest.
Arguments:
- tokens: bfloat16 [4, 1024, 512], P('hap', 'seq'), may hold values from -6 to 6
- cotangent: bfloat16 [4, 1024, 512], P('hap', 'seq'), may hold values from -6 to 6
- gaps: int32 [8, 2], P('seq'), may hold values from 0 to 128, as said below
- conv_taps: float32 [2, 3, 512], replicated, may hold values from -3.5 to 3.5
- norm_gains: float32 [2, 512], replicated, may hold values from 0.25 to 1.75
- projection: bfloat16 [2, 512, 1024], replicated, may hold values from -0.25 to 0.25
Outputs:
- tokens_grad: bfloat16 [4, 1024, 512], P('hap', 'seq')
- projection_grad: float32 [2, 512, 1024], P(None, 'seq')
- taps_grad: float32 [2, 3, 512], replicated
- gains_grad: float32 [2, 512], replicated
Inputs may be any that keep to these rules, and one draw needn't show every extreme that they name: `gaps`: each row holds a start and an end with start <= end; some run is wholly a gap and some has none; gap density varies from region to region.
All inputs are finite; a program needn't handle non-finite values.
Results may differ from a plain program's by a relative error of at most 0.0058.
Values may be sent and summed in bfloat16 or wider, within the bound.
A program may use at most 64 MiB of HBM per device.

v0:
```python
import jax
import jax.numpy as jnp
from jax import lax
from jax.sharding import PartitionSpec as P

DILATION_BINS = 32
LAYERS = 2


EPS = 1e-06


def extended(x, sides, width):
    for axis, dim in sides:
        devices, length = (lax.axis_size(axis), x.shape[dim])
        up = [(i, (i + 1) % devices) for i in range(devices - 1)]
        down = [(j, i) for i, j in up]
        last = lax.slice_in_dim(x, length - width, length, axis=dim)
        initial = lax.slice_in_dim(x, 0, width, axis=dim)
        before = lax.ppermute(last, axis, up)
        after = lax.ppermute(initial, axis, down)
        x = jnp.concatenate([before, x, after], axis=dim)
    return x


def valid_of(gap_rows):
    offsets = jnp.arange(128, dtype=jnp.int32)[None, :]
    inside = (offsets >= gap_rows[:, 0:1]) & (offsets < gap_rows[:, 1:2])
    return jnp.where(inside, 0.0, 1.0).astype(jnp.float32).reshape(-1)


def norm_part(inputs, valid, gain):
    scaled = inputs.astype(jnp.float32)
    inv_rms = lax.rsqrt(jnp.mean(scaled * scaled, axis=-1, keepdims=True) + EPS)
    return (scaled, inv_rms, scaled * inv_rms * gain * valid[:, None])


def project(preactivation, weight):
    hidden = jax.nn.gelu(preactivation).astype(jnp.bfloat16)
    proj_out = jnp.dot(hidden, weight, preferred_element_type=jnp.float32)
    halfway = weight.shape[1] // 2
    return (hidden, proj_out[:, :halfway], jax.nn.sigmoid(proj_out[:, halfway:]))


def convolve(filter_weight, padded_tracks, receptive_extent):
    return (
        filter_weight[0] * padded_tracks[0:receptive_extent]
        + filter_weight[1] * padded_tracks[DILATION_BINS : DILATION_BINS + receptive_extent]
        + filter_weight[2] * padded_tracks[2 * DILATION_BINS : 2 * DILATION_BINS + receptive_extent]
    )


def back_layer(grad, stored, valid, filter_weight, gain, weight):
    scaled, inv_rms, normalized_tracks, padded_tracks, preactivation, hidden, first, gate = stored
    local_bin_count = grad.shape[0]
    branch = valid[:, None] * grad
    dproj = jnp.concatenate([branch * gate, branch * first * gate * (1.0 - gate)], 1).astype(
        jnp.bfloat16
    )
    dhidden = lax.dot_general(
        dproj, weight, (((1,), (1,)), ((), ())), preferred_element_type=jnp.float32
    )
    proj_term = lax.dot_general(
        hidden, dproj, (((0,), (0,)), ((), ())), preferred_element_type=jnp.float32
    )
    preactivation_gradient = jax.vjp(jax.nn.gelu, preactivation)[1](dhidden)[0]
    wide_preactivation_gradient = extended(preactivation_gradient, (("seq", 0),), DILATION_BINS)
    normalized_gradient = (
        filter_weight[0] * wide_preactivation_gradient[2 * DILATION_BINS :]
        + filter_weight[1] * preactivation_gradient
        + filter_weight[2] * wide_preactivation_gradient[:local_bin_count]
    )
    tap_term = jnp.stack(
        [
            jnp.sum(preactivation_gradient * padded_tracks[:local_bin_count], 0),
            jnp.sum(preactivation_gradient * normalized_tracks, 0),
            jnp.sum(preactivation_gradient * padded_tracks[2 * DILATION_BINS :], 0),
        ]
    )
    dq = normalized_gradient * valid[:, None]
    gain_term = jnp.sum(dq * scaled * inv_rms, 0)
    dt = dq * gain
    grad = grad + inv_rms * dt - scaled * inv_rms**3 * jnp.mean(dt * scaled, axis=-1, keepdims=True)
    return (grad, proj_term, tap_term, gain_term)


def shards(tokens, cotangent, gaps, conv_taps, norm_gains, projection):
    features = tokens[0]
    local_bin_count = features.shape[0]
    valid = valid_of(gaps)
    stored_all = []
    current = features
    for layer in range(LAYERS):
        scaled, inv_rms, normalized_tracks = norm_part(current, valid, norm_gains[layer])
        padded_tracks = extended(normalized_tracks, (("seq", 0),), DILATION_BINS)
        preactivation = convolve(conv_taps[layer], padded_tracks, local_bin_count)
        hidden, first, gate = project(preactivation, projection[layer])
        current = (scaled + valid[:, None] * first * gate).astype(jnp.bfloat16)
        stored_all.append(
            (scaled, inv_rms, normalized_tracks, padded_tracks, preactivation, hidden, first, gate)
        )
    grad = cotangent[0].astype(jnp.float32)
    proj_terms = [None] * LAYERS
    filter_tap_products = [None] * LAYERS
    gain_terms = [None] * LAYERS
    for layer in reversed(range(LAYERS)):
        grad, proj_term, filter_tap_products[layer], gain_terms[layer] = back_layer(
            grad, stored_all[layer], valid, conv_taps[layer], norm_gains[layer], projection[layer]
        )
        proj_terms[layer] = proj_term
    stacked = jnp.stack(proj_terms)
    shared = lax.psum_scatter(stacked, "seq", scatter_dimension=1, tiled=True)
    projection_grad = lax.psum(shared, "hap")
    taps_grad, gains_grad = lax.psum(
        (jnp.stack(filter_tap_products), jnp.stack(gain_terms)), ("seq", "hap")
    )
    return (grad.astype(jnp.bfloat16)[None], projection_grad, taps_grad, gains_grad)


def solution(mesh):
    return jax.shard_map(
        shards,
        mesh=mesh,
        in_specs=(P("hap", "seq", None), P("hap", "seq", None), P("seq", None), P(), P(), P()),
        out_specs=(P("hap", "seq", None), P(None, "seq", None), P(), P()),
        check_vma=False,
    )
```

profile of v0, /device:TPU:0, one launch (start us, length us, event | category | flops | bytes accessed | tf_op | source)
XLA Modules:
  0.0 191.4 jit_solution(3818379955450865659)
XLA Ops:
  7.2 1.0 fusion.38
  8.3 1.3 fusion.81
  9.6 0.8 fusion.80
  10.4 1.3 multiply_multiply_fusion.4
  11.7 1.0 fusion.40
  12.7 5.0 %collective-permute-start = (f32[32,512]{1,0:T(8,128)S(1)}, f32[32,512]{1,0:T(8,128)S(1)}, u32[]{:S(2)}, u32[]{:S(2)}) collective-permute-start(f32[32,512]{1,0:T(8,128)S(1)} %get-tuple-element.38), channel_id=1, source_target_pairs={{0,4},{4,8},{8,12},{12,16},{16,20},{20,24},{24,28},{1,5},{5,9},{9,... | collective-permute-start | bytes 196616 | tf_op jit(solution)/shard_map/ppermute | solution.py:20
  17.7 1.3 collective-permute-start.1
  19.0 0.8 fusion.79
  19.8 4.1 %collective-permute-done.1 = f32[32,512]{1,0:T(8,128)S(1)} collective-permute-done((f32[32,512]{1,0:T(8,128)S(1)}, f32[32,512]{1,0:T(8,128)S(1)}, u32[]{:S(2)}, u32[]{:S(2)}) %collective-permute-start.1) | collective-permute-done | bytes 65568 | tf_op jit(solution)/shard_map/ppermute | solution.py:21
  23.9 1.6 fusion.6
  25.9 4.4 %collective-permute-start.2 = (f32[32,512]{1,0:T(8,128)S(1)}, f32[32,512]{1,0:T(8,128)S(1)}, u32[]{:S(2)}, u32[]{:S(2)}) collective-permute-start(f32[32,512]{1,0:T(8,128)S(1)} %get-tuple-element.36), channel_id=1, source_target_pairs={{0,4},{4,8},{8,12},{12,16},{16,20},{20,24},{24,28},{1,5},{5,9},{9,... | collective-permute-start | bytes 196616 | tf_op jit(solution)/shard_map/ppermute | solution.py:20
  30.2 1.3 collective-permute-start.3
  31.5 0.6 collective-permute-done.2
  32.1 4.3 %collective-permute-done.3 = f32[32,512]{1,0:T(8,128)S(1)} collective-permute-done((f32[32,512]{1,0:T(8,128)S(1)}, f32[32,512]{1,0:T(8,128)S(1)}, u32[]{:S(2)}, u32[]{:S(2)}) %collective-permute-start.3) | collective-permute-done | bytes 65568 | tf_op jit(solution)/shard_map/ppermute | solution.py:21
  36.4 0.4 fusion.2
  36.9 0.6 fusion.30
  37.6 1.3 collective-permute-start.4
  38.9 4.5 %collective-permute-start.5 = (f32[32,512]{1,0:T(8,128)S(1)}, f32[32,512]{1,0:T(8,128)S(1)}, u32[]{:S(2)}, u32[]{:S(2)}) collective-permute-start(f32[32,512]{1,0:T(8,128)S(1)} %get-tuple-element.35), channel_id=1, source_target_pairs={{0,4},{4,8},{8,12},{12,16},{16,20},{20,24},{24,28},{1,5},{5,9},{9,... | collective-permute-start | bytes 196616 | tf_op jit(solution)/shard_map/ppermute | solution.py:20
  43.4 0.5 convolution_bitcast_fusion
  43.9 1.4 collective-permute-done.5
  46.0 0.5 convolution_bitcast_fusion.1
  46.5 2.2 %pad_maximum_fusion = f32[2,512,1024]{2,1,0:T(8,128)} fusion(f32[1,512,1024]{2,1,0:T(8,128)S(1)} %convolution_bitcast_fusion, f32[1,512,1024]{2,1,0:T(8,128)S(1)} %convolution_bitcast_fusion.1), kind=kLoop, calls=%fused_computation | loop fusion | flops 1048576 | bytes 8388608 | tf_op jit(solution)/shard_map/stack | solution.py:111
  48.8 0.6 fusion.24
  49.4 1.3 collective-permute-start.6
  50.7 4.9 %collective-permute-start.7 = (f32[32,512]{1,0:T(8,128)S(1)}, f32[32,512]{1,0:T(8,128)S(1)}, u32[]{:S(2)}, u32[]{:S(2)}) collective-permute-start(f32[32,512]{1,0:T(8,128)S(1)} %get-tuple-element.33), channel_id=1, source_target_pairs={{0,4},{4,8},{8,12},{12,16},{16,20},{20,24},{24,28},{1,5},{5,9},{9,... | collective-permute-start | bytes 196616 | tf_op jit(solution)/shard_map/ppermute | solution.py:20
  55.7 0.3 collective-permute-done.6
  55.9 1.6 collective-permute-done.7
  57.8 82.7 %reduce-scatter.2.cloned.1.call-done = f32[2,64,1024]{2,1,0:T(8,128)} async-done(((f32[2,512,1024]{2,1,0:T(8,128)}), f32[2,64,1024]{2,1,0:T(8,128)}) %reduce-scatter.2.cloned.1.call-update) | async-done | bytes 524304 | tf_op jit(solution)/shard_map/reduce_scatter | solution.py:112
  140.5 40.8 %all-reduce = (f32[2,3,512]{2,1,0:T(4,128)S(1)}, f32[2,512]{1,0:T(2,128)}) all-reduce(f32[2,3,512]{2,1,0:T(4,128)S(1)} %pad_maximum_fusion.15, f32[2,512]{1,0:T(2,128)S(1)} %pad_maximum_fusion.16), channel_id=1, replica_groups=mesh['seq'=8,'hap'=4] {'seq','hap'}, use_global_device_ids=true, to_apply=%region_12.13 | all-reduce | flops 4096 | bytes 32768 | tf_op jit(solution)/shard_map/psum | solution.py:114
  181.3 0.6 copy.10
  181.9 0.8 fusion.68
  182.7 1.9 copy.12
  (31 shorter events, 1.6 us)
Async XLA Ops:
  7.2 18.3 %copy-start = (bf16[1,128,512]{2,1,0:T(8,128)(2,1)S(1)}, bf16[1,128,512]{2,1,0:T(8,128)(2,1)}, u32[]{:S(2)}) copy-start(bf16[1,128,512]{2,1,0:T(8,128)(2,1)} %param.6) | copy-start | bytes 393220
  7.2 133.3 %reduce-scatter.2.cloned.1.call-start = ((), (), s32[]{:S(2)}) async-start(), calls=%async_computation.1 | async-start | bytes 4718592 | tf_op jit(solution)/shard_map/reduce_scatter | solution.py:112
  12.7 23.7 %copy-start.2 = (bf16[2,512,1024]{2,1,0:T(8,128)(2,1)S(1)}, bf16[2,512,1024]{2,1,0:T(8,128)(2,1)}, u32[]{:S(2)}) copy-start(bf16[2,512,1024]{2,1,0:T(8,128)(2,1)} %param.11) | copy-start | bytes 6291460
  12.7 7.1 %collective-permute-start = (f32[32,512]{1,0:T(8,128)S(1)}, f32[32,512]{1,0:T(8,128)S(1)}, u32[]{:S(2)}, u32[]{:S(2)}) collective-permute-start(f32[32,512]{1,0:T(8,128)S(1)} %get-tuple-element.38), channel_id=1, source_target_pairs={{0,4},{4,8},{8,12},{12,16},{16,20},{20,24},{24,28},{1,5},{5,9},{9,... | collective-permute-start | bytes 196616 | tf_op jit(solution)/shard_map/ppermute | solution.py:20
  17.7 6.2 %collective-permute-start.1 = (f32[32,512]{1,0:T(8,128)S(1)}, f32[32,512]{1,0:T(8,128)S(1)}, u32[]{:S(2)}, u32[]{:S(2)}) collective-permute-start(f32[32,512]{1,0:T(8,128)S(1)} %get-tuple-element.39), channel_id=1, source_target_pairs={{4,0},{8,4},{12,8},{16,12},{20,16},{24,20},{28,24},{5,1},{9,5},{13... | collective-permute-start | bytes 196616 | tf_op jit(solution)/shard_map/ppermute | solution.py:21
  25.5 11.3 %copy-start.1 = (bf16[1,128,512]{2,1,0:T(8,128)(2,1)S(1)}, bf16[1,128,512]{2,1,0:T(8,128)(2,1)}, u32[]{:S(2)}) copy-start(bf16[1,128,512]{2,1,0:T(8,128)(2,1)} %param.7) | copy-start | bytes 393220
  25.9 6.2 %collective-permute-start.2 = (f32[32,512]{1,0:T(8,128)S(1)}, f32[32,512]{1,0:T(8,128)S(1)}, u32[]{:S(2)}, u32[]{:S(2)}) collective-permute-start(f32[32,512]{1,0:T(8,128)S(1)} %get-tuple-element.36), channel_id=1, source_target_pairs={{0,4},{4,8},{8,12},{12,16},{16,20},{20,24},{24,28},{1,5},{5,9},{9,... | collective-permute-start | bytes 196616 | tf_op jit(solution)/shard_map/ppermute | solution.py:20
  30.2 6.2 %collective-permute-start.3 = (f32[32,512]{1,0:T(8,128)S(1)}, f32[32,512]{1,0:T(8,128)S(1)}, u32[]{:S(2)}, u32[]{:S(2)}) collective-permute-start(f32[32,512]{1,0:T(8,128)S(1)} %get-tuple-element.37), channel_id=1, source_target_pairs={{4,0},{8,4},{12,8},{16,12},{20,16},{24,20},{28,24},{5,1},{9,5},{13... | collective-permute-start | bytes 196616 | tf_op jit(solution)/shard_map/ppermute | solution.py:21
  37.6 6.4 %collective-permute-start.4 = (f32[32,512]{1,0:T(8,128)S(1)}, f32[32,512]{1,0:T(8,128)S(1)}, u32[]{:S(2)}, u32[]{:S(2)}) collective-permute-start(f32[32,512]{1,0:T(8,128)S(1)} %get-tuple-element.34), channel_id=1, source_target_pairs={{4,0},{8,4},{12,8},{16,12},{20,16},{24,20},{28,24},{5,1},{9,5},{13... | collective-permute-start | bytes 196616 | tf_op jit(solution)/shard_map/ppermute | solution.py:21
  38.9 6.4 %collective-permute-start.5 = (f32[32,512]{1,0:T(8,128)S(1)}, f32[32,512]{1,0:T(8,128)S(1)}, u32[]{:S(2)}, u32[]{:S(2)}) collective-permute-start(f32[32,512]{1,0:T(8,128)S(1)} %get-tuple-element.35), channel_id=1, source_target_pairs={{0,4},{4,8},{8,12},{12,16},{16,20},{20,24},{24,28},{1,5},{5,9},{9,... | collective-permute-start | bytes 196616 | tf_op jit(solution)/shard_map/ppermute | solution.py:20
  48.7 134.0 %all-reduce.3.cloned.1.call-start = ((), (), s32[]{:S(2)}) async-start(), calls=%async_computation.2 | async-start | bytes 1048576 | tf_op jit(solution)/shard_map/psum | solution.py:113
  49.4 6.5 %collective-permute-start.6 = (f32[32,512]{1,0:T(8,128)S(1)}, f32[32,512]{1,0:T(8,128)S(1)}, u32[]{:S(2)}, u32[]{:S(2)}) collective-permute-start(f32[32,512]{1,0:T(8,128)S(1)} %get-tuple-element.32), channel_id=1, source_target_pairs={{4,0},{8,4},{12,8},{16,12},{20,16},{24,20},{28,24},{5,1},{9,5},{13... | collective-permute-start | bytes 196616 | tf_op jit(solution)/shard_map/ppermute | solution.py:21
  50.7 6.8 %collective-permute-start.7 = (f32[32,512]{1,0:T(8,128)S(1)}, f32[32,512]{1,0:T(8,128)S(1)}, u32[]{:S(2)}, u32[]{:S(2)}) collective-permute-start(f32[32,512]{1,0:T(8,128)S(1)} %get-tuple-element.33), channel_id=1, source_target_pairs={{0,4},{4,8},{8,12},{12,16},{16,20},{20,24},{24,28},{1,5},{5,9},{9,... | collective-permute-start | bytes 196616 | tf_op jit(solution)/shard_map/ppermute | solution.py:20
Sparse Core Ops, SparseCore 0:
  48.8 91.6 reduce-scatter.1
  143.0 32.9 all-reduce.2
where the time goes:
time: 192 us; the launch traced here: 191 us
  waiting for transfers between devices  94.9 us (49%)
  blocking collectives  40.8 us (21%)
  starting transfers between devices  24.1 us (13%)
  between operations  14.3 us (7%)
  other arithmetic  7.83 us (4%)
  local copies, waits for them, and re-layouts  5.43 us (3%)
  matrix products  4.2 us (2%)
    reduce_scatter x1, waiting for transfers between devices, shards(): shared = lax.psum_scatter(stacked, 'seq', scatter_dimension=1, tiled=True)  82.7 us
    psum x1, blocking collectives, shards(): lax.psum((jnp.stack(filter_tap_products), jnp.stack(gain_terms)), ('seq',...  40.8 us
    ppermute x4, starting transfers between devices, extended(): before = lax.ppermute(last, axis, up)  18.8 us
    ppermute x4, waiting for transfers between devices, extended(): after = lax.ppermute(initial, axis, down)  8.62 us
    ppermute x4, starting transfers between devices, extended(): after = lax.ppermute(initial, axis, down)  5.17 us
  transfers between devices with their start and end apart: 10, of which 7 were waited for; matrix products, arithmetic and copies ran while one was open for 2% of the time, Pallas kernels for 0%

commit v1 on v0

v1 whole, which is shorter than its diff:
```python
import functools

import jax
import jax.numpy as jnp
from jax import lax
from jax.experimental import pallas as pl
from jax.experimental.pallas import tpu as pltpu
from jax.sharding import PartitionSpec as P

D = 32
LAYERS = 2
EPS = 1e-06
GELU_C = 0.7978845608028654
GELU_A = 0.044715
F32 = jnp.float32
BF16 = jnp.bfloat16
MESH = pl.DeviceIdType.MESH


def kernel(
    n, haps, inside,
    tok, cot, gaps, taps, gains, w_hbm,
    tg_out, pg_out, sm_out,
    w, wsem, edge_out, halo_in, hs, hr, xs, inv, npad, dgelu, hid, proj, dp, dpad, gcur,
    hT, hTs, hTr, dq_in, dqs, dqr, gbf, rs, rss, rsr, ag, ags, agr, smh, smhs, smhr, sms, smss, smsr,
):
    me, h = lax.axis_index("seq"), lax.axis_index("hap")
    N, C = tok.shape
    PR = w.shape[2]
    Q = PR // haps
    chunks = N // D
    outer, inner = (0, chunks - 1), tuple(range(1, chunks - 1))
    rows = C // n
    left, right = jnp.maximum(me - 1, 0), jnp.minimum(me + 1, n - 1)
    has_left, has_right = me > 0, me < n - 1
    sends = []

    loads = [pltpu.make_async_copy(w_hbm.at[l], w.at[l], wsem.at[l]) for l in range(LAYERS)]
    for c in loads:
        c.start()

    barrier = pltpu.get_barrier_semaphore()
    if inside:
        for d in range(1, n):
            pl.semaphore_signal(barrier, inc=1, device_id={"seq": lax.rem(me + d, n)}, device_id_type=MESH)
        for d in range(1, haps):
            pl.semaphore_signal(barrier, inc=1, device_id={"hap": lax.rem(h + d, haps)}, device_id_type=MESH)
    else:
        @pl.when(has_left)
        def _():
            pl.semaphore_signal(barrier, inc=1, device_id={"seq": left}, device_id_type=MESH)

        @pl.when(has_right)
        def _():
            pl.semaphore_signal(barrier, inc=1, device_id={"seq": right}, device_id_type=MESH)

    offs = lax.broadcasted_iota(jnp.int32, (D, 1), 0)

    def valid_of(i):
        b = offs + i * D
        return jnp.where((b >= gaps[0, 0]) & (b < gaps[0, 1]), 0.0, 1.0).astype(F32)

    valid = [valid_of(i) for i in range(chunks)]

    def ds(i):
        return pl.ds(i * D, D)

    def halo(k):
        up = pltpu.make_async_remote_copy(
            src_ref=edge_out.at[k, 1], dst_ref=halo_in.at[k, 0], send_sem=hs.at[k, 1],
            recv_sem=hr.at[k, 0], device_id={"seq": right}, device_id_type=MESH)
        down = pltpu.make_async_remote_copy(
            src_ref=edge_out.at[k, 0], dst_ref=halo_in.at[k, 1], send_sem=hs.at[k, 0],
            recv_sem=hr.at[k, 1], device_id={"seq": left}, device_id_type=MESH)
        return up, down

    def halo_start(k):
        up, down = halo(k)

        @pl.when(has_right)
        def _():
            up.start()

        @pl.when(has_left)
        def _():
            down.start()

        @pl.when(jnp.logical_not(has_left))
        def _():
            halo_in[k, 0] = jnp.zeros((D, C), BF16)

        @pl.when(jnp.logical_not(has_right))
        def _():
            halo_in[k, 1] = jnp.zeros((D, C), BF16)

    def halo_wait(k):
        up, down = halo(k)

        @pl.when(has_left)
        def _():
            up.wait_recv()

        @pl.when(has_right)
        def _():
            down.wait_recv()

    def halo_drain(k):
        up, down = halo(k)

        @pl.when(has_right)
        def _():
            up.wait_send()

        @pl.when(has_left)
        def _():
            down.wait_send()

    def to_hap(src_of, dst_of, ss, rr):
        out = []
        for d in range(1, haps):
            t = lax.rem(h + d, haps)
            c = pltpu.make_async_remote_copy(
                src_ref=src_of(t), dst_ref=dst_of(d), send_sem=ss(d), recv_sem=rr(d),
                device_id={"hap": t}, device_id_type=MESH)
            c.start()
            out.append(c)
        sends.extend(out)
        return out

    def to_seq(src_of, dst_of, ss, rr):
        out = []
        for d in range(1, n):
            t = lax.rem(me + d, n)
            c = pltpu.make_async_remote_copy(
                src_ref=src_of(t), dst_ref=dst_of(d), send_sem=ss(d), recv_sem=rr(d),
                device_id={"seq": t}, device_id_type=MESH)
            c.start()
            out.append(c)
        sends.extend(out)
        return out

    xs[0] = tok[...]
    edge_out[0, 0] = (tok[ds(0), :].astype(F32) * valid[0]).astype(BF16)
    edge_out[0, 1] = (tok[ds(chunks - 1), :].astype(F32) * valid[-1]).astype(BF16)
    if inside:
        pl.semaphore_wait(barrier, n - 1 + haps - 1)
    else:
        @pl.when(has_left)
        def _():
            pl.semaphore_wait(barrier, 1)

        @pl.when(has_right)
        def _():
            pl.semaphore_wait(barrier, 1)
    halo_start(0)

    def rms(x):
        return lax.rsqrt(jnp.mean(x * x, axis=-1, keepdims=True) + EPS)

    def forward_chunk(l, i):
        pre = (
            taps[l, 0:1, :] * npad[l, ds(i), :]
            + taps[l, 1:2, :] * npad[l, ds(i + 1), :]
            + taps[l, 2:3, :] * npad[l, ds(i + 2), :]
        )
        sq = pre * pre
        th = jnp.tanh(GELU_C * (pre + GELU_A * (sq * pre)))
        half = 0.5 * (1.0 + th)
        hidden = (pre * half).astype(BF16)
        hid[l, ds(i), :] = hidden
        dgelu[l, ds(i), :] = half + 0.5 * pre * (1.0 - th * th) * (GELU_C * (1.0 + 3.0 * GELU_A * sq))

    hT_copies = [None] * LAYERS
    for l in range(LAYERS):
        gain = gains[l : l + 1, :]
        for i in range(chunks):
            x = xs[l, ds(i), :].astype(F32)
            r = rms(x)
            inv[l, ds(i), :] = r
            npad[l, ds(i + 1), :] = x * r * gain * valid[i]
        for i in inner:
            forward_chunk(l, i)
        halo_wait(l)
        for side, at in ((0, 0), (1, chunks + 1)):
            x = halo_in[l, side].astype(F32)
            npad[l, ds(at), :] = x * rms(x) * gain
        for i in outer:
            forward_chunk(l, i)
        loads[l].wait()
        proj[l] = jnp.dot(hid[l], w[l], preferred_element_type=F32)
        if l + 1 < LAYERS:
            for i in outer + inner:
                first = proj[l, ds(i), 0:C]
                gate = jax.nn.sigmoid(proj[l, ds(i), C:PR])
                proj[l, ds(i), C:PR] = gate
                nxt = (xs[l, ds(i), :].astype(F32) + valid[i] * first * gate).astype(BF16)
                xs[l + 1, ds(i), :] = nxt
                if i in outer:
                    edge_out[l + 1, 0 if i == 0 else 1] = (nxt.astype(F32) * valid[i]).astype(BF16)
                if i == outer[-1]:
                    halo_start(l + 1)
        hT[l, :, 0:N] = jnp.transpose(hid[l].astype(F32)).astype(BF16)
        if inside:
            hT_copies[l] = to_hap(
                lambda t: hT.at[l, :, pl.ds(0, N)], lambda d: hT.at[l, :, pl.ds(d * N, N)],
                lambda d: hTs.at[l, d], lambda d: hTr.at[l, d])

    dq_copies, rs_copies, ag_copies = [None] * LAYERS, [None] * LAYERS, [None] * LAYERS

    def gram(l):
        if not inside:
            pg_out[l] = jnp.dot(hT[l], dp[l], preferred_element_type=F32)
            return
        dq_in[l, 0:N, :] = dp[l, :, pl.ds(pl.multiple_of(h * Q, Q), Q)]
        for c in hT_copies[l] + dq_copies[l]:
            c.wait_recv()
        g = jnp.dot(hT[l], dq_in[l], preferred_element_type=F32)
        gbf[l] = g.astype(BF16).reshape(n, rows, Q)
        rs_copies[l] = to_seq(
            lambda t: gbf.at[l, t], lambda d: rs.at[l, d], lambda d: rss.at[l, d], lambda d: rsr.at[l, d])

    def reduced(l):
        total = gbf[l, me].astype(F32)
        for c in rs_copies[l]:
            c.wait_recv()
        for d in range(1, n):
            total = total + rs[l, d].astype(F32)
        ag[l, h] = total.astype(BF16)
        ag_copies[l] = to_hap(
            lambda t: ag.at[l, h], lambda d: ag.at[l, h], lambda d: ags.at[l, d], lambda d: agr.at[l, d])

    for l in reversed(range(LAYERS)):
        k = 2 * LAYERS - 1 - l
        last = l == LAYERS - 1
        gain = gains[l : l + 1, :]
        for i in range(chunks):
            first = proj[l, ds(i), 0:C]
            gate = proj[l, ds(i), C:PR]
            if last:
                gate = jax.nn.sigmoid(gate)
            grad = cot[ds(i), :].astype(F32) if last else gcur[ds(i), :]
            branch = valid[i] * grad
            bg = branch * gate
            dp[l, ds(i), 0:C] = bg.astype(BF16)
            dp[l, ds(i), C:PR] = (bg * first * (1.0 - gate)).astype(BF16)
        if inside:
            dq_copies[l] = to_hap(
                lambda t: dp.at[l, :, pl.ds(pl.multiple_of(t * Q, Q), Q)],
                lambda d: dq_in.at[l, pl.ds(d * N, N), :],
                lambda d: dqs.at[l, d], lambda d: dqr.at[l, d])
        dpad[l, pl.ds(D, N), :] = lax.dot_general(
            dp[l], w[l], (((1,), (1,)), ((), ())), preferred_element_type=F32)
        t_sum = [jnp.zeros((1, C), F32) for _ in range(3)]
        for i in outer + inner:
            dpre = dpad[l, ds(i + 1), :] * dgelu[l, ds(i), :]
            dpad[l, ds(i + 1), :] = dpre
            if i in outer:
                edge_out[k, 0 if i == 0 else 1] = dpre.astype(BF16)
            if i == outer[-1]:
                halo_start(k)
            for j in range(3):
                t_sum[j] = t_sum[j] + jnp.sum(dpre * npad[l, ds(i + j), :], axis=0, keepdims=True)
        g_sum = jnp.zeros((1, C), F32)

        def back_chunk(i, g_sum):
            dn = (
                taps[l, 0:1, :] * dpad[l, ds(i + 2), :]
                + taps[l, 1:2, :] * dpad[l, ds(i + 1), :]
                + taps[l, 2:3, :] * dpad[l, ds(i), :]
            )
            dq = dn * valid[i]
            x = xs[l, ds(i), :].astype(F32)
            r = inv[l, ds(i), :]
            xr = x * r
            g_sum = g_sum + jnp.sum(dq * xr, axis=0, keepdims=True)
            dt = dq * gain
            grad = cot[ds(i), :].astype(F32) if last else gcur[ds(i), :]
            new = grad + r * dt - xr * (r * r * jnp.mean(dt * x, axis=-1, keepdims=True))
            if l == 0:
                tg_out[ds(i), :] = new
            else:
                gcur[ds(i), :] = new
            return g_sum

        for i in inner:
            g_sum = back_chunk(i, g_sum)
        gram(l)
        halo_wait(k)
        dpad[l, ds(0), :] = halo_in[k, 0].astype(F32)
        dpad[l, ds(chunks + 1), :] = halo_in[k, 1].astype(F32)
        for i in outer:
            g_sum = back_chunk(i, g_sum)
        for j in range(3):
            smh[h, 3 * l + j : 3 * l + j + 1, :] = t_sum[j]
        smh[h, 3 * LAYERS + l : 3 * LAYERS + l + 1, :] = g_sum

    if inside:
        small = to_hap(lambda t: smh.at[h], lambda d: smh.at[h], lambda d: smhs.at[d], lambda d: smhr.at[d])
        reduced(LAYERS - 1)
        for c in small:
            c.wait_recv()
        total = smh[0]
        for q in range(1, haps):
            total = total + smh[q]
        sms[me] = total
        small = to_seq(lambda t: sms.at[me], lambda d: sms.at[me], lambda d: smss.at[d], lambda d: smsr.at[d])
        for l in reversed(range(LAYERS - 1)):
            reduced(l)
        for c in small:
            c.wait_recv()
        total = sms[0]
        for s in range(1, n):
            total = total + sms[s]
        sm_out[...] = total
        for l in reversed(range(LAYERS)):
            for c in ag_copies[l]:
                c.wait_recv()
            for q in range(haps):
                pg_out[l, :, q * Q : (q + 1) * Q] = ag[l, q]
    else:
        sm_out[...] = smh[h]
    for k in range(2 * LAYERS):
        halo_drain(k)
    for c in sends:
        c.wait_send()


def shards(n, haps, tokens, cotangent, gaps, conv_taps, norm_gains, projection):
    x = tokens[0]
    N, C = x.shape
    PR = projection.shape[2]
    inside = n > 1 and haps > 1 and C % (16 * n) == 0 and PR % (128 * haps) == 0
    Q, rows = PR // haps, max(C // n, 1)
    L = LAYERS
    wide = haps if inside else 1

    def dma(*shape):
        return pltpu.SemaphoreType.DMA(shape)

    def opt(shape, dtype):
        return pltpu.VMEM(shape if inside else (16, 128), dtype)

    scratch = [
        pltpu.VMEM((L, C, PR), BF16), dma(L),
        pltpu.VMEM((2 * L, 2, D, C), BF16), pltpu.VMEM((2 * L, 2, D, C), BF16), dma(2 * L, 2), dma(2 * L, 2),
        pltpu.VMEM((L, N, C), BF16), pltpu.VMEM((L, N, 1), F32), pltpu.VMEM((L, N + 2 * D, C), F32),
        pltpu.VMEM((L, N, C), F32), pltpu.VMEM((L, N, C), BF16), pltpu.VMEM((L, N, PR), F32),
        pltpu.VMEM((L, N, PR), BF16), pltpu.VMEM((L, N + 2 * D, C), F32), pltpu.VMEM((N, C), F32),
        pltpu.VMEM((L, C, N * wide), BF16), dma(L, haps), dma(L, haps),
        opt((L, N * haps, Q), BF16), dma(L, haps), dma(L, haps),
        opt((L, n, rows, Q), BF16), opt((L, n, rows, Q), BF16), dma(L, n), dma(L, n),
        opt((L, haps, rows, Q), BF16), dma(L, haps), dma(L, haps),
        pltpu.VMEM((haps, 4 * L, C), F32), dma(haps), dma(haps),
        opt((n, 4 * L, C), F32), dma(n), dma(n),
    ]
    vmem = pl.BlockSpec(memory_space=pltpu.VMEM)
    pg_shape = jax.ShapeDtypeStruct((L, rows, PR), BF16) if inside else jax.ShapeDtypeStruct((L, C, PR), F32)
    tg, pg, sm = pl.pallas_call(
        functools.partial(kernel, n, haps, inside),
        out_shape=[jax.ShapeDtypeStruct((N, C), F32), pg_shape, jax.ShapeDtypeStruct((4 * L, C), F32)],
        in_specs=[vmem, vmem, pl.BlockSpec(memory_space=pltpu.SMEM), vmem, vmem, pl.BlockSpec(memory_space=pl.ANY)],
        out_specs=[vmem] * 3,
        scratch_shapes=scratch,
        compiler_params=pltpu.CompilerParams(
            collective_id=0, has_side_effects=True, vmem_limit_bytes=48 * 1024 * 1024),
    )(x, cotangent[0], gaps, conv_taps, norm_gains, projection)
    if inside:
        pg = pg.astype(F32)
    else:
        pg = lax.psum(lax.psum_scatter(pg, "seq", scatter_dimension=1, tiled=True), "hap")
        sm = lax.psum(sm, ("seq", "hap"))
    return tg.astype(BF16)[None], pg, sm[: 3 * L].reshape(L, 3, C), sm[3 * L :]


def solution(mesh):
    return jax.shard_map(
        functools.partial(shards, mesh.shape["seq"], mesh.shape["hap"]),
        mesh=mesh,
        in_specs=(P("hap", "seq", None), P("hap", "seq", None), P("seq", None), P(), P(), P()),
        out_specs=(P("hap", "seq", None), P(None, "seq", None), P(), P()),
        check_vma=False,
    )
```

time: 192 us -> 51.7 us (0.27)
  waiting for transfers between devices: 94.9 us -> 0 us
  Pallas kernels: 0 us -> 42.6 us
  blocking collectives: 40.8 us -> 0 us
  starting transfers between devices: 24.1 us -> 0 us
  between operations: 14.3 us -> 0.65 us
  other arithmetic: 7.83 us -> 1.52 us
  matrix products: 4.2 us -> 0 us
    reduce_scatter x1 -> x0, waiting for transfers between devices: 82.7 us -> none  [shards(): shared = lax.psum_scatter(stacked, 'seq', scatter_dimension=1, tiled=True)]
    pallas_call x0 -> x1, Pallas kernels: none -> 42.6 us  [shards(): pl.pallas_call(functools.partial(kernel, n, haps, inside), out_shape=[jax...]
    psum x1 -> x0, blocking collectives: 40.8 us -> none  [shards(): lax.psum((jnp.stack(filter_tap_products), jnp.stack(gain_terms)), ('seq',...]
    ppermute x8 -> x0, starting transfers between devices: 24 us -> none  [the longest x4 18.8 us: extended(): before = lax.ppermute(last, axis, up)]
    ppermute x8 -> x0, waiting for transfers between devices: 12.2 us -> none  [the longest x4 8.62 us: extended(): after = lax.ppermute(initial, axis, down)]
    dot_general x6 -> x0, matrix products: 4.2 us -> none  [the longest x2 2 us: project(): proj_out = jnp.dot(hidden, weight, preferred_element_type=jnp.float32)]
    unnamed x8 -> x12, local copies, waits for them, and re-layouts: 2.51 us -> 6.06 us
    another operation x8 -> x0, other arithmetic: 2.78 us -> none  [the longest x1 2.23 us: shards(): stacked = jnp.stack(proj_terms)]
  transfers between devices with their start and end apart: 10 -> 0, of which waited for: 7 -> 0; matrix products, arithmetic and copies ran while one was open for 2% -> 0% of each run, Pallas kernels for 0% -> 0%
where the time goes in v1:
time: 51.7 us; the launch traced here: 51.4 us
  Pallas kernels  42.6 us (82%)
  local copies, waits for them, and re-layouts  6.66 us (13%)
  other arithmetic  1.52 us (3%)
  between operations  0.65 us (1%)
    pallas_call x1, Pallas kernels, shards(): pl.pallas_call(functools.partial(kernel, n, haps, inside), out_shape=[jax...  42.6 us
    unnamed x12, local copies, waits for them, and re-layouts  6.06 us

profile of v1, /device:TPU:0, one launch (start us, length us, event | category | flops | bytes accessed | tf_op | source)
XLA Modules:
  0.0 51.4 jit_solution(1473967666218723885)
XLA Ops:
  0.6 0.7 %copy.12.taps = f32[2,3,512]{2,1,0:T(4,128)S(1)} copy(f32[2,3,512]{2,0,1:T(2,128)} %param.9) | data formatting | bytes 24576 | tf_op args[3]
  1.3 0.0 copy-start
  1.3 1.6 %copy-done = bf16[2,512,1024]{2,1,0:T(8,128)(2,1)S(1)} copy-done((bf16[2,512,1024]{2,1,0:T(8,128)(2,1)S(1)}, bf16[2,512,1024]{2,1,0:T(8,128)(2,1)}, u32[]{:S(2)}) %copy-start) | copy-done | bytes 2097176
  2.9 0.0 copy-start.1
  2.9 0.9 %copy-done.1 = bf16[1,128,512]{2,1,0:T(8,128)(2,1)S(1)} copy-done((bf16[1,128,512]{2,1,0:T(8,128)(2,1)S(1)}, bf16[1,128,512]{2,1,0:T(8,128)(2,1)}, u32[]{:S(2)}) %copy-start.1) | copy-done | bytes 131096
  3.8 0.0 copy-start.2
  3.8 0.9 %copy-done.2 = bf16[1,128,512]{2,1,0:T(8,128)(2,1)S(1)} copy-done((bf16[1,128,512]{2,1,0:T(8,128)(2,1)S(1)}, bf16[1,128,512]{2,1,0:T(8,128)(2,1)}, u32[]{:S(2)}) %copy-start.2) | copy-done | bytes 131096
  4.7 0.0 copy-start.3
  4.7 0.7 %copy-done.3 = f32[2,512]{1,0:T(2,128)S(1)} copy-done((f32[2,512]{1,0:T(2,128)S(1)}, f32[2,512]{1,0:T(2,128)}, u32[]{:S(2)}) %copy-start.3) | copy-done | bytes 4120
  5.4 0.0 copy-start.4
  5.4 0.7 %copy-done.4 = s32[1,2]{1,0:T(1,128)S(1)} copy-done((s32[1,2]{1,0:T(1,128)S(1)}, s32[1,2]{1,0:T(1,128)}, u32[]{:S(2)}) %copy-start.4) | copy-done | bytes 32
  6.1 42.6 %shard_map.93 = (f32[128,512]{1,0:T(8,128)S(1)}, bf16[2,64,1024]{2,1,0:T(8,128)(2,1)S(1)}, f32[8,512]{1,0:T(8,128)S(1)}) custom-call(bf16[128,512]{1,0:T(8,128)(2,1)S(1)} %bitcast.5, bf16[128,512]{1,0:T(8,128)(2,1)S(1)} %bitcast.6, s32[1,2]{1,0:T(1,128)S(1)} %copy-done.4, f32[2,3,512]{2,1,0:T(4,128)S(1)} %copy.12.taps, f32[2,512]{1,0:T(2,128)S(1)} %copy-done.3, ...), custom_call_target="tpu_custom_call" | custom-call | tf_op jit(solution)/shard_map/pallas_call | solution.py:358
  48.7 0.7 %convert_bitcast_fusion = bf16[1,128,512]{2,1,0:T(8,128)(2,1)} fusion(f32[128,512]{1,0:T(8,128)S(1)} %get-tuple-element.7), kind=kLoop, calls=%fused_computation | loop fusion | flops 65536 | bytes 393216 | tf_op jit(solution)/shard_map/broadcast_in_dim | solution.py:372
  49.4 0.6 %slice.7 = f32[2,512]{1,0:T(2,128)} slice(f32[8,512]{1,0:T(8,128)S(1)} %get-tuple-element.9), slice={[6:8], [0:512]} | slice | bytes 8192 | tf_op jit(solution)/shard_map/slice | solution.py:372
  50.0 0.6 %copy.13 = f32[2,3,512]{2,0,1:T(2,128)} copy(f32[2,3,512]{2,1,0:T(4,128)S(1)} %reshape.11) | data formatting | bytes 24576
  50.6 0.8 %convert_element_type.7 = f32[2,64,1024]{2,1,0:T(8,128)} convert(bf16[2,64,1024]{2,1,0:T(8,128)(2,1)S(1)} %get-tuple-element.8) | non-fusion elementwise | flops 131072 | bytes 786432 | tf_op jit(solution)/shard_map/convert_element_type | solution.py:368
  (1 shorter events, 0.0 us)
Async XLA Ops:
  1.3 1.6 %copy-start = (bf16[2,512,1024]{2,1,0:T(8,128)(2,1)S(1)}, bf16[2,512,1024]{2,1,0:T(8,128)(2,1)}, u32[]{:S(2)}) copy-start(bf16[2,512,1024]{2,1,0:T(8,128)(2,1)} %w_hbm.1) | copy-start | bytes 6291460
  2.9 0.9 %copy-start.1 = (bf16[1,128,512]{2,1,0:T(8,128)(2,1)S(1)}, bf16[1,128,512]{2,1,0:T(8,128)(2,1)}, u32[]{:S(2)}) copy-start(bf16[1,128,512]{2,1,0:T(8,128)(2,1)} %param.6) | copy-start | bytes 393220
  3.8 0.9 %copy-start.2 = (bf16[1,128,512]{2,1,0:T(8,128)(2,1)S(1)}, bf16[1,128,512]{2,1,0:T(8,128)(2,1)}, u32[]{:S(2)}) copy-start(bf16[1,128,512]{2,1,0:T(8,128)(2,1)} %param.7) | copy-start | bytes 393220
  4.7 0.7 %copy-start.3 = (f32[2,512]{1,0:T(2,128)S(1)}, f32[2,512]{1,0:T(2,128)}, u32[]{:S(2)}) copy-start(f32[2,512]{1,0:T(2,128)} %gains.1) | copy-start | bytes 12292
  5.4 0.7 %copy-start.4 = (s32[1,2]{1,0:T(1,128)S(1)}, s32[1,2]{1,0:T(1,128)}, u32[]{:S(2)}) copy-start(s32[1,2]{1,0:T(1,128)} %gaps.1) | copy-start | bytes 28

commit v2 on v1

--- a/solution.py
+++ b/solution.py
@@ -19,9 +19,9 @@
 
 def kernel(
     n, haps, inside,
-    tok, cot, gaps, taps, gains, w_hbm,
+    tok_hbm, cot_hbm, gaps_hbm, taps_hbm, gains_hbm, w_hbm,
     tg_out, pg_out, sm_out,
-    w, wsem, edge_out, halo_in, hs, hr, xs, inv, npad, dgelu, hid, proj, dp, dpad, gcur,
+    tok, cot, gaps, taps, gains, isem, w, wsem, edge_out, halo_in, hs, hr, xs, inv, npad, dgelu, hid, proj, dp, dpad, gcur,
     hT, hTs, hTr, dq_in, dqs, dqr, gbf, rs, rss, rsr, ag, ags, agr, smh, smhs, smhr, sms, smss, smsr,
 ):
     me, h = lax.axis_index("seq"), lax.axis_index("hap")
@@ -36,7 +36,12 @@
     sends = []
 
     loads = [pltpu.make_async_copy(w_hbm.at[l], w.at[l], wsem.at[l]) for l in range(LAYERS)]
-    for c in loads:
+    small_in = [
+        pltpu.make_async_copy(a, b, isem.at[j])
+        for j, (a, b) in enumerate(
+            ((tok_hbm, tok), (gaps_hbm, gaps), (gains_hbm, gains), (taps_hbm, taps), (cot_hbm, cot)))
+    ]
+    for c in small_in[:4] + loads + small_in[4:]:
         c.start()
 
     barrier = pltpu.get_barrier_semaphore()
@@ -60,6 +65,8 @@
         b = offs + i * D
         return jnp.where((b >= gaps[0, 0]) & (b < gaps[0, 1]), 0.0, 1.0).astype(F32)
 
+    small_in[0].wait()
+    small_in[1].wait()
     valid = [valid_of(i) for i in range(chunks)]
 
     def ds(i):
@@ -153,15 +160,17 @@
         def _():
             pl.semaphore_wait(barrier, 1)
     halo_start(0)
+    small_in[2].wait()
+    small_in[3].wait()
 
     def rms(x):
         return lax.rsqrt(jnp.mean(x * x, axis=-1, keepdims=True) + EPS)
 
     def forward_chunk(l, i):
         pre = (
-            taps[l, 0:1, :] * npad[l, ds(i), :]
-            + taps[l, 1:2, :] * npad[l, ds(i + 1), :]
-            + taps[l, 2:3, :] * npad[l, ds(i + 2), :]
+            taps[0, l : l + 1, :] * npad[l, ds(i), :]
+            + taps[1, l : l + 1, :] * npad[l, ds(i + 1), :]
+            + taps[2, l : l + 1, :] * npad[l, ds(i + 2), :]
         )
         sq = pre * pre
         th = jnp.tanh(GELU_C * (pre + GELU_A * (sq * pre)))
@@ -171,6 +180,14 @@
         dgelu[l, ds(i), :] = half + 0.5 * pre * (1.0 - th * th) * (GELU_C * (1.0 + 3.0 * GELU_A * sq))
 
     hT_copies = [None] * LAYERS
+
+    def send_hidden(l):
+        hT[l, :, 0:N] = jnp.transpose(hid[l].astype(F32)).astype(BF16)
+        if inside:
+            hT_copies[l] = to_hap(
+                lambda t: hT.at[l, :, pl.ds(0, N)], lambda d: hT.at[l, :, pl.ds(d * N, N)],
+                lambda d: hTs.at[l, d], lambda d: hTr.at[l, d])
+
     for l in range(LAYERS):
         gain = gains[l : l + 1, :]
         for i in range(chunks):
@@ -199,13 +216,10 @@
                     edge_out[l + 1, 0 if i == 0 else 1] = (nxt.astype(F32) * valid[i]).astype(BF16)
                 if i == outer[-1]:
                     halo_start(l + 1)
-        hT[l, :, 0:N] = jnp.transpose(hid[l].astype(F32)).astype(BF16)
-        if inside:
-            hT_copies[l] = to_hap(
-                lambda t: hT.at[l, :, pl.ds(0, N)], lambda d: hT.at[l, :, pl.ds(d * N, N)],
-                lambda d: hTs.at[l, d], lambda d: hTr.at[l, d])
-
-    dq_copies, rs_copies, ag_copies = [None] * LAYERS, [None] * LAYERS, [None] * LAYERS
+        if l + 1 < LAYERS:
+            send_hidden(l)
+
+    dq_copies, rs_copies, ag_copies = [[] for _ in range(LAYERS)], [None] * LAYERS, [None] * LAYERS
 
     def gram(l):
         if not inside:
@@ -229,28 +243,39 @@
         ag_copies[l] = to_hap(
             lambda t: ag.at[l, h], lambda d: ag.at[l, h], lambda d: ags.at[l, d], lambda d: agr.at[l, d])
 
+    def dproj(l, i):
+        last = l == LAYERS - 1
+        first = proj[l, ds(i), 0:C]
+        gate = proj[l, ds(i), C:PR]
+        if last:
+            gate = jax.nn.sigmoid(gate)
+        grad = cot[ds(i), :].astype(F32) if last else gcur[ds(i), :]
+        bg = valid[i] * grad * gate
+        dp[l, ds(i), 0:C] = bg.astype(BF16)
+        dp[l, ds(i), C:PR] = (bg * first * (1.0 - gate)).astype(BF16)
+
+    def send_dproj(l, j, start, size):
+        if inside:
+            dq_copies[l] += to_hap(
+                lambda t: dp.at[l, pl.ds(start, size), pl.ds(pl.multiple_of(t * Q, Q), Q)],
+                lambda d: dq_in.at[l, pl.ds(d * N + start, size), :],
+                lambda d: dqs.at[l, d, j], lambda d: dqr.at[l, d, j])
+
+    def fold(x):
+        return jnp.sum(x.reshape(D // 8, 8, C), axis=0)
+
+    small_in[4].wait()
+    for i in range(chunks):
+        dproj(LAYERS - 1, i)
+    send_dproj(LAYERS - 1, 0, 0, N)
     for l in reversed(range(LAYERS)):
         k = 2 * LAYERS - 1 - l
         last = l == LAYERS - 1
         gain = gains[l : l + 1, :]
-        for i in range(chunks):
-            first = proj[l, ds(i), 0:C]
-            gate = proj[l, ds(i), C:PR]
-            if last:
-                gate = jax.nn.sigmoid(gate)
-            grad = cot[ds(i), :].astype(F32) if last else gcur[ds(i), :]
-            branch = valid[i] * grad
-            bg = branch * gate
-            dp[l, ds(i), 0:C] = bg.astype(BF16)
-            dp[l, ds(i), C:PR] = (bg * first * (1.0 - gate)).astype(BF16)
-        if inside:
-            dq_copies[l] = to_hap(
-                lambda t: dp.at[l, :, pl.ds(pl.multiple_of(t * Q, Q), Q)],
-                lambda d: dq_in.at[l, pl.ds(d * N, N), :],
-                lambda d: dqs.at[l, d], lambda d: dqr.at[l, d])
+        if not last:
+            gram(l + 1)
         dpad[l, pl.ds(D, N), :] = lax.dot_general(
             dp[l], w[l], (((1,), (1,)), ((), ())), preferred_element_type=F32)
-        t_sum = [jnp.zeros((1, C), F32) for _ in range(3)]
         for i in outer + inner:
             dpre = dpad[l, ds(i + 1), :] * dgelu[l, ds(i), :]
             dpad[l, ds(i + 1), :] = dpre
@@ -258,41 +283,53 @@
                 edge_out[k, 0 if i == 0 else 1] = dpre.astype(BF16)
             if i == outer[-1]:
                 halo_start(k)
-            for j in range(3):
-                t_sum[j] = t_sum[j] + jnp.sum(dpre * npad[l, ds(i + j), :], axis=0, keepdims=True)
-        g_sum = jnp.zeros((1, C), F32)
+        if last:
+            send_hidden(l)
+        g_sum = jnp.zeros((8, C), F32)
 
         def back_chunk(i, g_sum):
             dn = (
-                taps[l, 0:1, :] * dpad[l, ds(i + 2), :]
-                + taps[l, 1:2, :] * dpad[l, ds(i + 1), :]
-                + taps[l, 2:3, :] * dpad[l, ds(i), :]
+                taps[0, l : l + 1, :] * dpad[l, ds(i + 2), :]
+                + taps[1, l : l + 1, :] * dpad[l, ds(i + 1), :]
+                + taps[2, l : l + 1, :] * dpad[l, ds(i), :]
             )
             dq = dn * valid[i]
             x = xs[l, ds(i), :].astype(F32)
             r = inv[l, ds(i), :]
             xr = x * r
-            g_sum = g_sum + jnp.sum(dq * xr, axis=0, keepdims=True)
+            g_sum = g_sum + fold(dq * xr)
             dt = dq * gain
             grad = cot[ds(i), :].astype(F32) if last else gcur[ds(i), :]
             new = grad + r * dt - xr * (r * r * jnp.mean(dt * x, axis=-1, keepdims=True))
             if l == 0:
-                tg_out[ds(i), :] = new
+                tg_out[ds(i), :] = new.astype(BF16)
             else:
                 gcur[ds(i), :] = new
+                dproj(l - 1, i)
             return g_sum
 
         for i in inner:
             g_sum = back_chunk(i, g_sum)
-        gram(l)
+        if l > 0:
+            send_dproj(l - 1, 0, D, N - 2 * D)
+        t_sum = [jnp.zeros((8, C), F32) for _ in range(3)]
+        for i in range(chunks):
+            dpre = dpad[l, ds(i + 1), :]
+            for j in range(3):
+                t_sum[j] = t_sum[j] + fold(dpre * npad[l, ds(i + j), :])
+        for j in range(3):
+            smh[h, LAYERS * j + l : LAYERS * j + l + 1, :] = jnp.sum(t_sum[j], axis=0, keepdims=True)
+        if l == 0:
+            gram(0)
         halo_wait(k)
         dpad[l, ds(0), :] = halo_in[k, 0].astype(F32)
         dpad[l, ds(chunks + 1), :] = halo_in[k, 1].astype(F32)
         for i in outer:
             g_sum = back_chunk(i, g_sum)
-        for j in range(3):
-            smh[h, 3 * l + j : 3 * l + j + 1, :] = t_sum[j]
-        smh[h, 3 * LAYERS + l : 3 * LAYERS + l + 1, :] = g_sum
+        if l > 0:
+            send_dproj(l - 1, 1, 0, D)
+            send_dproj(l - 1, 2, N - D, D)
+        smh[h, 3 * LAYERS + l : 3 * LAYERS + l + 1, :] = jnp.sum(g_sum, axis=0, keepdims=True)
 
     if inside:
         small = to_hap(lambda t: smh.at[h], lambda d: smh.at[h], lambda d: smhs.at[d], lambda d: smhr.at[d])
@@ -325,6 +362,15 @@
         c.wait_send()
 
 
+def finish(tg, pg, sm, tg_out, pg_out, taps_out, gains_out):
+    L, C = gains_out.shape
+    tg_out[...] = tg[...]
+    pg_out[...] = pg[...].astype(F32)
+    for j in range(3):
+        taps_out[j] = sm[j * L : (j + 1) * L, :]
+    gains_out[...] = sm[3 * L :, :]
+
+
 def shards(n, haps, tokens, cotangent, gaps, conv_taps, norm_gains, projection):
     x = tokens[0]
     N, C = x.shape
@@ -341,35 +387,45 @@
         return pltpu.VMEM(shape if inside else (16, 128), dtype)
 
     scratch = [
+        pltpu.VMEM((N, C), BF16), pltpu.VMEM((N, C), BF16), pltpu.SMEM(gaps.shape, jnp.int32),
+        pltpu.VMEM((3, L, C), F32), pltpu.VMEM((L, C), F32), dma(5),
         pltpu.VMEM((L, C, PR), BF16), dma(L),
         pltpu.VMEM((2 * L, 2, D, C), BF16), pltpu.VMEM((2 * L, 2, D, C), BF16), dma(2 * L, 2), dma(2 * L, 2),
         pltpu.VMEM((L, N, C), BF16), pltpu.VMEM((L, N, 1), F32), pltpu.VMEM((L, N + 2 * D, C), F32),
         pltpu.VMEM((L, N, C), F32), pltpu.VMEM((L, N, C), BF16), pltpu.VMEM((L, N, PR), F32),
         pltpu.VMEM((L, N, PR), BF16), pltpu.VMEM((L, N + 2 * D, C), F32), pltpu.VMEM((N, C), F32),
         pltpu.VMEM((L, C, N * wide), BF16), dma(L, haps), dma(L, haps),
-        opt((L, N * haps, Q), BF16), dma(L, haps), dma(L, haps),
+        opt((L, N * haps, Q), BF16), dma(L, haps, 3), dma(L, haps, 3),
         opt((L, n, rows, Q), BF16), opt((L, n, rows, Q), BF16), dma(L, n), dma(L, n),
         opt((L, haps, rows, Q), BF16), dma(L, haps), dma(L, haps),
         pltpu.VMEM((haps, 4 * L, C), F32), dma(haps), dma(haps),
         opt((n, 4 * L, C), F32), dma(n), dma(n),
     ]
     vmem = pl.BlockSpec(memory_space=pltpu.VMEM)
+    hbm = pl.BlockSpec(memory_space=pltpu.HBM)
     pg_shape = jax.ShapeDtypeStruct((L, rows, PR), BF16) if inside else jax.ShapeDtypeStruct((L, C, PR), F32)
     tg, pg, sm = pl.pallas_call(
         functools.partial(kernel, n, haps, inside),
-        out_shape=[jax.ShapeDtypeStruct((N, C), F32), pg_shape, jax.ShapeDtypeStruct((4 * L, C), F32)],
-        in_specs=[vmem, vmem, pl.BlockSpec(memory_space=pltpu.SMEM), vmem, vmem, pl.BlockSpec(memory_space=pl.ANY)],
+        out_shape=[jax.ShapeDtypeStruct((N, C), BF16), pg_shape, jax.ShapeDtypeStruct((4 * L, C), F32)],
+        in_specs=[hbm] * 6,
         out_specs=[vmem] * 3,
         scratch_shapes=scratch,
         compiler_params=pltpu.CompilerParams(
-            collective_id=0, has_side_effects=True, vmem_limit_bytes=48 * 1024 * 1024),
-    )(x, cotangent[0], gaps, conv_taps, norm_gains, projection)
-    if inside:
-        pg = pg.astype(F32)
-    else:
+            collective_id=0, has_side_effects=True, vmem_limit_bytes=60 * 1024 * 1024),
+    )(x, cotangent[0], gaps, jnp.transpose(conv_taps, (1, 0, 2)), norm_gains, projection)
+    if not inside:
         pg = lax.psum(lax.psum_scatter(pg, "seq", scatter_dimension=1, tiled=True), "hap")
         sm = lax.psum(sm, ("seq", "hap"))
-    return tg.astype(BF16)[None], pg, sm[: 3 * L].reshape(L, 3, C), sm[3 * L :]
+    tg, pg, taps, gains = pl.pallas_call(
+        finish,
+        out_shape=[
+            jax.ShapeDtypeStruct(tg.shape, BF16), jax.ShapeDtypeStruct(pg.shape, F32),
+            jax.ShapeDtypeStruct((3, L, C), F32), jax.ShapeDtypeStruct((L, C), F32)],
+        in_specs=[vmem] * 3,
+        out_specs=[vmem] * 4,
+        compiler_params=pltpu.CompilerParams(vmem_limit_bytes=8 * 1024 * 1024),
+    )(tg, pg, sm)
+    return tg[None], pg, jnp.transpose(taps, (1, 0, 2)), gains
 
 
 def solution(mesh):

time: 51.7 us -> 49.3 us (0.954)
  local copies, waits for them, and re-layouts: 6.66 us -> 2.56 us
  Pallas kernels: 42.6 us -> 45.8 us
  other arithmetic: 1.52 us -> 0 us
    unnamed x12 -> x6, local copies, waits for them, and re-layouts: 6.06 us -> 2.56 us
    pallas_call x1, Pallas kernels: 42.6 us -> 45 us  [shards(): pl.pallas_call(functools.partial(kernel, n, haps, inside), out_shape=[jax...]
    pallas_call x0 -> x1, Pallas kernels: none -> 0.88 us  [shards(): pl.pallas_call(finish, out_shape=[jax.ShapeDtypeStruct(tg.shape, BF16), j...]
    convert_element_type x1 -> x0, other arithmetic: 0.84 us -> none  [shards(): pg = pg.astype(F32)]
    broadcast_in_dim x1 -> x0, other arithmetic: 0.67 us -> none  [shards(): return (tg.astype(BF16)[None], pg, sm[:3 * L].reshape(L, 3, C), sm[3 * L:])]
    slice x1 -> x0, local copies, waits for them, and re-layouts: 0.6 us -> none  [shards(): return (tg.astype(BF16)[None], pg, sm[:3 * L].reshape(L, 3, C), sm[3 * L:])]
where the time goes in v2:
time: 49.3 us; the launch traced here: 49.1 us
  Pallas kernels  45.8 us (93%)
  local copies, waits for them, and re-layouts  2.56 us (5%)
  between operations  0.65 us (1%)
    pallas_call x1, Pallas kernels, shards(): pl.pallas_call(functools.partial(kernel, n, haps, inside), out_shape=[jax...  45 us
    unnamed x6, local copies, waits for them, and re-layouts  2.56 us

profile of v2, /device:TPU:0, one launch (start us, length us, event | category | flops | bytes accessed | tf_op | source)
XLA Modules:
  0.0 49.1 jit_solution(1237759905407436261)
XLA Ops:
  0.6 45.0 %shard_map.93 = (bf16[128,512]{1,0:T(8,128)(2,1)}, bf16[2,64,1024]{2,1,0:T(8,128)(2,1)}, f32[8,512]{1,0:T(8,128)}) custom-call(bf16[128,512]{1,0:T(8,128)(2,1)} %bitcast.5, bf16[128,512]{1,0:T(8,128)(2,1)} %bitcast.6, s32[1,2]{1,0:T(1,128)} %gaps_hbm.1, f32[3,2,512]{2,1,0:T(2,128)} %bitcast.7, f32[2,512]{1,0:T(2,128)} %gains_hbm.1, bf16[2,512,1024]{2,1,0:T(8,128)(2,1)} %w_hbm.1), custom_call_target="tpu_custom_call" | custom-call | tf_op jit(solution)/shard_map/pallas_call | solution.py:407
  45.6 0.0 copy-start
  45.6 0.9 %copy-done = bf16[2,64,1024]{2,1,0:T(8,128)(2,1)S(1)} copy-done((bf16[2,64,1024]{2,1,0:T(8,128)(2,1)S(1)}, bf16[2,64,1024]{2,1,0:T(8,128)(2,1)}, u32[]{:S(2)}) %copy-start) | copy-done | bytes 262168
  46.6 0.0 copy-start.1
  46.6 0.9 %copy-done.1 = bf16[128,512]{1,0:T(8,128)(2,1)S(1)} copy-done((bf16[128,512]{1,0:T(8,128)(2,1)S(1)}, bf16[128,512]{1,0:T(8,128)(2,1)}, u32[]{:S(2)}) %copy-start.1) | copy-done | bytes 131096
  47.5 0.0 copy-start.2
  47.5 0.7 %copy-done.2 = f32[8,512]{1,0:T(8,128)S(1)} copy-done((f32[8,512]{1,0:T(8,128)S(1)}, f32[8,512]{1,0:T(8,128)}, u32[]{:S(2)}) %copy-start.2) | copy-done | bytes 16408
  48.2 0.9 %shard_map.94 = (bf16[128,512]{1,0:T(8,128)(2,1)}, f32[2,64,1024]{2,1,0:T(8,128)}, f32[3,2,512]{2,1,0:T(2,128)}, f32[2,512]{1,0:T(2,128)}) custom-call(bf16[128,512]{1,0:T(8,128)(2,1)S(1)} %copy-done.1, bf16[2,64,1024]{2,1,0:T(8,128)(2,1)S(1)} %copy-done, f32[8,512]{1,0:T(8,128)S(1)} %copy-done.2), custom_call_target="tpu_custom_call" | custom-call | tf_op jit(solution)/shard_map/pallas_call | solution.py:419
Async XLA Ops:
  45.6 1.0 %copy-start = (bf16[2,64,1024]{2,1,0:T(8,128)(2,1)S(1)}, bf16[2,64,1024]{2,1,0:T(8,128)(2,1)}, u32[]{:S(2)}) copy-start(bf16[2,64,1024]{2,1,0:T(8,128)(2,1)} %get-tuple-element.12.pg) | copy-start | bytes 786436
  46.6 0.9 %copy-start.1 = (bf16[128,512]{1,0:T(8,128)(2,1)S(1)}, bf16[128,512]{1,0:T(8,128)(2,1)}, u32[]{:S(2)}) copy-start(bf16[128,512]{1,0:T(8,128)(2,1)} %get-tuple-element.11.tg) | copy-start | bytes 393220
  47.5 0.7 %copy-start.2 = (f32[8,512]{1,0:T(8,128)S(1)}, f32[8,512]{1,0:T(8,128)}, u32[]{:S(2)}) copy-start(f32[8,512]{1,0:T(8,128)} %get-tuple-element.13.sm) | copy-start | bytes 49156

commit v3 on v2

--- a/solution.py
+++ b/solution.py
@@ -20,8 +20,8 @@
 def kernel(
     n, haps, inside,
     tok_hbm, cot_hbm, gaps_hbm, taps_hbm, gains_hbm, w_hbm,
-    tg_out, pg_out, sm_out,
-    tok, cot, gaps, taps, gains, isem, w, wsem, edge_out, halo_in, hs, hr, xs, inv, npad, dgelu, hid, proj, dp, dpad, gcur,
+    tg_hbm, pg_hbm, tp_hbm, gn_hbm,
+    tg_out, pg_out, tp_out, gn_out, osem, tok, cot, gaps, taps, gains, isem, w, wsem, edge_out, halo_in, hs, hr, xs, inv, npad, dgelu, hid, proj, dp, dpad, gcur,
     hT, hTs, hTr, dq_in, dqs, dqr, gbf, rs, rss, rsr, ag, ags, agr, smh, smhs, smhr, sms, smss, smsr,
 ):
     me, h = lax.axis_index("seq"), lax.axis_index("hap")
@@ -122,10 +122,13 @@
         def _():
             down.wait_send()
 
-    def to_hap(src_of, dst_of, ss, rr):
+    core = h + 1 - 2 * lax.rem(h, 2)
+    peers = (h, core, lax.rem(h + 2, haps), lax.rem(core + 2, haps))
+
+    def to_hap(src_of, dst_of, ss, rr, which=(1, 2, 3), to=None):
         out = []
-        for d in range(1, haps):
-            t = lax.rem(h + d, haps)
+        for d in which:
+            t = peers[d if to is None else to]
             c = pltpu.make_async_remote_copy(
                 src_ref=src_of(t), dst_ref=dst_of(d), send_sem=ss(d), recv_sem=rr(d),
                 device_id={"hap": t}, device_id_type=MESH)
@@ -186,8 +189,25 @@
         if inside:
             hT_copies[l] = to_hap(
                 lambda t: hT.at[l, :, pl.ds(0, N)], lambda d: hT.at[l, :, pl.ds(d * N, N)],
-                lambda d: hTs.at[l, d], lambda d: hTr.at[l, d])
-
+                lambda d: hTs.at[l, d], lambda d: hTr.at[l, d], (1, 2))
+
+    def relay_hidden(l):
+        if inside:
+            hT_copies[l][1].wait_recv()
+            hT_copies[l] = [hT_copies[l][0]] + to_hap(
+                lambda t: hT.at[l, :, pl.ds(2 * N, N)], lambda d: hT.at[l, :, pl.ds(d * N, N)],
+                lambda d: hTs.at[l, d], lambda d: hTr.at[l, d], (3,), 1)
+
+    def start_out(l):
+        for c in ag_copies[l]:
+            c.wait_recv()
+        for q in range(haps):
+            pg_out[l, :, q * Q : (q + 1) * Q] = ag[l, q].astype(F32)
+        c = pltpu.make_async_copy(pg_out.at[l], pg_hbm.at[l], osem.at[3 + l])
+        c.start()
+        outs.append(c)
+
+    outs = []
     for l in range(LAYERS):
         gain = gains[l : l + 1, :]
         for i in range(chunks):
@@ -203,12 +223,14 @@
             npad[l, ds(at), :] = x * rms(x) * gain
         for i in outer:
             forward_chunk(l, i)
+        if l + 1 == LAYERS:
+            send_hidden(l)
         loads[l].wait()
         proj[l] = jnp.dot(hid[l], w[l], preferred_element_type=F32)
         if l + 1 < LAYERS:
             for i in outer + inner:
                 first = proj[l, ds(i), 0:C]
-                gate = jax.nn.sigmoid(proj[l, ds(i), C:PR])
+                gate = 0.5 + 0.5 * jnp.tanh(0.5 * proj[l, ds(i), C:PR])
                 proj[l, ds(i), C:PR] = gate
                 nxt = (xs[l, ds(i), :].astype(F32) + valid[i] * first * gate).astype(BF16)
                 xs[l + 1, ds(i), :] = nxt
@@ -248,7 +270,7 @@
         first = proj[l, ds(i), 0:C]
         gate = proj[l, ds(i), C:PR]
         if last:
-            gate = jax.nn.sigmoid(gate)
+            gate = 0.5 + 0.5 * jnp.tanh(0.5 * gate)
         grad = cot[ds(i), :].astype(F32) if last else gcur[ds(i), :]
         bg = valid[i] * grad * gate
         dp[l, ds(i), 0:C] = bg.astype(BF16)
@@ -265,6 +287,8 @@
         return jnp.sum(x.reshape(D // 8, 8, C), axis=0)
 
     small_in[4].wait()
+    for l in range(LAYERS - 1):
+        relay_hidden(l)
     for i in range(chunks):
         dproj(LAYERS - 1, i)
     send_dproj(LAYERS - 1, 0, 0, N)
@@ -283,8 +307,6 @@
                 edge_out[k, 0 if i == 0 else 1] = dpre.astype(BF16)
             if i == outer[-1]:
                 halo_start(k)
-        if last:
-            send_hidden(l)
         g_sum = jnp.zeros((8, C), F32)
 
         def back_chunk(i, g_sum):
@@ -322,6 +344,8 @@
         if l == 0:
             gram(0)
         halo_wait(k)
+        if last:
+            relay_hidden(l)
         dpad[l, ds(0), :] = halo_in[k, 0].astype(F32)
         dpad[l, ds(chunks + 1), :] = halo_in[k, 1].astype(F32)
         for i in outer:
@@ -331,9 +355,13 @@
             send_dproj(l - 1, 2, N - D, D)
         smh[h, 3 * LAYERS + l : 3 * LAYERS + l + 1, :] = jnp.sum(g_sum, axis=0, keepdims=True)
 
+    c = pltpu.make_async_copy(tg_out, tg_hbm, osem.at[0])
+    c.start()
+    outs.append(c)
     if inside:
         small = to_hap(lambda t: smh.at[h], lambda d: smh.at[h], lambda d: smhs.at[d], lambda d: smhr.at[d])
-        reduced(LAYERS - 1)
+        for l in range(1, LAYERS):
+            reduced(l)
         for c in small:
             c.wait_recv()
         total = smh[0]
@@ -341,41 +369,52 @@
             total = total + smh[q]
         sms[me] = total
         small = to_seq(lambda t: sms.at[me], lambda d: sms.at[me], lambda d: smss.at[d], lambda d: smsr.at[d])
-        for l in reversed(range(LAYERS - 1)):
-            reduced(l)
+        reduced(0)
+        for l in range(1, LAYERS):
+            start_out(l)
         for c in small:
             c.wait_recv()
         total = sms[0]
-        for s in range(1, n):
-            total = total + sms[s]
-        sm_out[...] = total
-        for l in reversed(range(LAYERS)):
-            for c in ag_copies[l]:
-                c.wait_recv()
-            for q in range(haps):
-                pg_out[l, :, q * Q : (q + 1) * Q] = ag[l, q]
+        for q in range(1, n):
+            total = total + sms[q]
     else:
-        sm_out[...] = smh[h]
+        total = smh[h]
+        for l in range(LAYERS):
+            c = pltpu.make_async_copy(pg_out.at[l], pg_hbm.at[l], osem.at[3 + l])
+            c.start()
+            outs.append(c)
+    for j in range(3):
+        tp_out[j] = total[j * LAYERS : (j + 1) * LAYERS, :]
+    gn_out[...] = total[3 * LAYERS :, :]
+    for c in (pltpu.make_async_copy(tp_out, tp_hbm, osem.at[1]), pltpu.make_async_copy(gn_out, gn_hbm, osem.at[2])):
+        c.start()
+        outs.append(c)
+    if inside:
+        start_out(0)
     for k in range(2 * LAYERS):
         halo_drain(k)
     for c in sends:
         c.wait_send()
-
-
-def finish(tg, pg, sm, tg_out, pg_out, taps_out, gains_out):
-    L, C = gains_out.shape
-    tg_out[...] = tg[...]
-    pg_out[...] = pg[...].astype(F32)
-    for j in range(3):
-        taps_out[j] = sm[j * L : (j + 1) * L, :]
-    gains_out[...] = sm[3 * L :, :]
+    for c in outs:
+        c.wait()
+
+
+def finish(a, b, c, d, a_out, b_out, c_out, d_out, sem):
+    copies = [
+        pltpu.make_async_copy(x, y, sem.at[j])
+        for j, (x, y) in enumerate(((b, b_out), (a, a_out), (c, c_out), (d, d_out)))
+    ]
+    for x in copies:
+        x.start()
+    for x in copies:
+        x.wait()
 
 
 def shards(n, haps, tokens, cotangent, gaps, conv_taps, norm_gains, projection):
     x = tokens[0]
     N, C = x.shape
     PR = projection.shape[2]
-    inside = n > 1 and haps > 1 and C % (16 * n) == 0 and PR % (128 * haps) == 0
+    inside = n > 1 and haps == 4 and C % (16 * n) == 0 and PR % (128 * haps) == 0
     Q, rows = PR // haps, max(C // n, 1)
     L = LAYERS
     wide = haps if inside else 1
@@ -401,30 +440,32 @@
         pltpu.VMEM((haps, 4 * L, C), F32), dma(haps), dma(haps),
         opt((n, 4 * L, C), F32), dma(n), dma(n),
     ]
-    vmem = pl.BlockSpec(memory_space=pltpu.VMEM)
     hbm = pl.BlockSpec(memory_space=pltpu.HBM)
-    pg_shape = jax.ShapeDtypeStruct((L, rows, PR), BF16) if inside else jax.ShapeDtypeStruct((L, C, PR), F32)
-    tg, pg, sm = pl.pallas_call(
+    outs = [
+        jax.ShapeDtypeStruct((N, C), BF16), jax.ShapeDtypeStruct((L, rows if inside else C, PR), F32),
+        jax.ShapeDtypeStruct((3, L, C), F32), jax.ShapeDtypeStruct((L, C), F32)]
+    scratch = [pltpu.VMEM(o.shape, o.dtype) for o in outs] + [dma(3 + L)] + scratch
+    params = dict(vmem_limit_bytes=60 * 1024 * 1024)
+    tg, pg, taps, gains = pl.pallas_call(
         functools.partial(kernel, n, haps, inside),
-        out_shape=[jax.ShapeDtypeStruct((N, C), BF16), pg_shape, jax.ShapeDtypeStruct((4 * L, C), F32)],
+        out_shape=outs,
         in_specs=[hbm] * 6,
-        out_specs=[vmem] * 3,
+        out_specs=[hbm] * 4,
         scratch_shapes=scratch,
-        compiler_params=pltpu.CompilerParams(
-            collective_id=0, has_side_effects=True, vmem_limit_bytes=60 * 1024 * 1024),
+        compiler_params=pltpu.CompilerParams(collective_id=0, has_side_effects=True, **params),
     )(x, cotangent[0], gaps, jnp.transpose(conv_taps, (1, 0, 2)), norm_gains, projection)
-    if not inside:
+    if inside:
+        tg, pg, taps, gains = pl.pallas_call(
+            finish,
+            out_shape=outs,
+            in_specs=[hbm] * 4,
+            out_specs=[hbm] * 4,
+            scratch_shapes=[dma(4)],
+            compiler_params=pltpu.CompilerParams(**params),
+        )(tg, pg, taps, gains)
+    else:
         pg = lax.psum(lax.psum_scatter(pg, "seq", scatter_dimension=1, tiled=True), "hap")
-        sm = lax.psum(sm, ("seq", "hap"))
-    tg, pg, taps, gains = pl.pallas_call(
-        finish,
-        out_shape=[
-            jax.ShapeDtypeStruct(tg.shape, BF16), jax.ShapeDtypeStruct(pg.shape, F32),
-            jax.ShapeDtypeStruct((3, L, C), F32), jax.ShapeDtypeStruct((L, C), F32)],
-        in_specs=[vmem] * 3,
-        out_specs=[vmem] * 4,
-        compiler_params=pltpu.CompilerParams(vmem_limit_bytes=8 * 1024 * 1024),
-    )(tg, pg, sm)
+        taps, gains = lax.psum((taps, gains), ("seq", "hap"))
     return tg[None], pg, jnp.transpose(taps, (1, 0, 2)), gains
 
 

time: 49.3 us -> 62.6 us (1.27)
  Pallas kernels: 45.8 us -> 61.9 us
  local copies, waits for them, and re-layouts: 2.56 us -> 0 us
    pallas_call x2, Pallas kernels: 45.8 us -> 61.9 us  [the longest x1 40.4 us: shards(): pl.pallas_call(functools.partial(kernel, n, haps, inside), out_shape=outs...]
    unnamed x6 -> x0, local copies, waits for them, and re-layouts: 2.56 us -> none
where the time goes in v3:
time: 62.6 us; the launch traced here: 62.5 us
  Pallas kernels  61.9 us (99%)
  between operations  0.64 us (1%)
    pallas_call x1, Pallas kernels, shards(): pl.pallas_call(functools.partial(kernel, n, haps, inside), out_shape=outs...  40.4 us
    pallas_call x1, Pallas kernels, shards(): pl.pallas_call(finish, out_shape=outs, in_specs=[hbm] * 4, out_specs=[hbm...  21.5 us

profile of v3, /device:TPU:0, one launch (start us, length us, event | category | flops | bytes accessed | tf_op | source)
XLA Modules:
  0.0 62.5 jit_solution(14171395098706875521)
XLA Ops:
  0.6 40.4 %shard_map.93 = (bf16[128,512]{1,0:T(8,128)(2,1)}, f32[2,64,1024]{2,1,0:T(8,128)}, f32[3,2,512]{2,1,0:T(2,128)}, f32[2,512]{1,0:T(2,128)}) custom-call(bf16[128,512]{1,0:T(8,128)(2,1)} %bitcast.5, bf16[128,512]{1,0:T(8,128)(2,1)} %bitcast.6, s32[1,2]{1,0:T(1,128)} %gaps_hbm.1, f32[3,2,512]{2,1,0:T(2,128)} %bitcast.7, f32[2,512]{1,0:T(2,128)} %gains_hbm.1, ...), custom_call_target="tpu_custom_call" | custom-call | tf_op jit(solution)/shard_map/pallas_call | solution.py:449
  41.0 21.5 %shard_map.94 = (bf16[128,512]{1,0:T(8,128)(2,1)}, f32[2,64,1024]{2,1,0:T(8,128)}, f32[3,2,512]{2,1,0:T(2,128)}, f32[2,512]{1,0:T(2,128)}) custom-call(bf16[128,512]{1,0:T(8,128)(2,1)} %get-tuple-element.12.a, f32[2,64,1024]{2,1,0:T(8,128)} %get-tuple-element.13.b, f32[3,2,512]{2,1,0:T(2,128)} %get-tuple-element.14.c, f32[2,512]{1,0:T(2,128)} %get-tuple-element.15.d), custom_call_target="tpu_custom_call" | custom-call | tf_op jit(solution)/shard_map/pallas_call | solution.py:458

commit v4 on v3

--- a/solution.py
+++ b/solution.py
@@ -22,12 +22,12 @@
     tok_hbm, cot_hbm, gaps_hbm, taps_hbm, gains_hbm, w_hbm,
     tg_hbm, pg_hbm, tp_hbm, gn_hbm,
     tg_out, pg_out, tp_out, gn_out, osem, tok, cot, gaps, taps, gains, isem, w, wsem, edge_out, halo_in, hs, hr, xs, inv, npad, dgelu, hid, proj, dp, dpad, gcur,
-    hT, hTs, hTr, dq_in, dqs, dqr, gbf, rs, rss, rsr, ag, ags, agr, smh, smhs, smhr, sms, smss, smsr,
+    hT, hTs, hTr, dq_in, dqs, dqr, gbf, xr, xrs, xrr, own, zb, zr, zrs, zrr, ag, ags, agr, sml, smh, smhs, smhr, sms, smss, smsr, sma, smas, smar,
 ):
     me, h = lax.axis_index("seq"), lax.axis_index("hap")
     N, C = tok.shape
     PR = w.shape[2]
-    Q = PR // haps
+    Q, Cq = PR // haps, C // haps
     chunks = N // D
     outer, inner = (0, chunks - 1), tuple(range(1, chunks - 1))
     rows = C // n
@@ -241,7 +241,10 @@
         if l + 1 < LAYERS:
             send_hidden(l)
 
-    dq_copies, rs_copies, ag_copies = [[] for _ in range(LAYERS)], [None] * LAYERS, [None] * LAYERS
+    dq_copies, x_copies, z_copies, ag_copies = [[[] for _ in range(LAYERS)] for _ in range(4)]
+    nz = n // 2
+    z, x = me // 2, lax.rem(me, 2)
+    order = [nz // 2] + [j for j in range(1, nz) if j != nz // 2] + [0]
 
     def gram(l):
         if not inside:
@@ -252,15 +255,36 @@
             c.wait_recv()
         g = jnp.dot(hT[l], dq_in[l], preferred_element_type=F32)
         gbf[l] = g.astype(BF16).reshape(n, rows, Q)
-        rs_copies[l] = to_seq(
-            lambda t: gbf.at[l, t], lambda d: rs.at[l, d], lambda d: rss.at[l, d], lambda d: rsr.at[l, d])
+        for j in order:
+            c = pltpu.make_async_remote_copy(
+                src_ref=gbf.at[l, 2 * lax.rem(z + j, nz) + 1 - x], dst_ref=xr.at[l, j],
+                send_sem=xrs.at[l, j], recv_sem=xrr.at[l, j],
+                device_id={"seq": 2 * z + 1 - x}, device_id_type=MESH)
+            c.start()
+            x_copies[l].append(c)
+        sends.extend(x_copies[l])
+
+    def forward(l):
+        for j, c in zip(order, x_copies[l]):
+            t = 2 * lax.rem(z + j, nz) + x
+            c.wait_recv()
+            total = gbf[l, t].astype(F32) + xr[l, j].astype(F32)
+            if j == 0:
+                own[l] = total
+                continue
+            zb[l, j] = total.astype(BF16)
+            c = pltpu.make_async_remote_copy(
+                src_ref=zb.at[l, j], dst_ref=zr.at[l, j], send_sem=zrs.at[l, j], recv_sem=zrr.at[l, j],
+                device_id={"seq": t}, device_id_type=MESH)
+            c.start()
+            z_copies[l].append((j, c))
+            sends.append(c)
 
     def reduced(l):
-        total = gbf[l, me].astype(F32)
-        for c in rs_copies[l]:
-            c.wait_recv()
-        for d in range(1, n):
-            total = total + rs[l, d].astype(F32)
+        total = own[l]
+        for j, c in z_copies[l]:
+            c.wait_recv()
+            total = total + zr[l, j].astype(F32)
         ag[l, h] = total.astype(BF16)
         ag_copies[l] = to_hap(
             lambda t: ag.at[l, h], lambda d: ag.at[l, h], lambda d: ags.at[l, d], lambda d: agr.at[l, d])
@@ -340,8 +364,11 @@
             for j in range(3):
                 t_sum[j] = t_sum[j] + fold(dpre * npad[l, ds(i + j), :])
         for j in range(3):
-            smh[h, LAYERS * j + l : LAYERS * j + l + 1, :] = jnp.sum(t_sum[j], axis=0, keepdims=True)
+            sml[LAYERS * j + l : LAYERS * j + l + 1, :] = jnp.sum(t_sum[j], axis=0, keepdims=True)
         if l == 0:
+            if inside:
+                for m in range(1, LAYERS):
+                    forward(m)
             gram(0)
         halo_wait(k)
         if last:
@@ -353,15 +380,19 @@
         if l > 0:
             send_dproj(l - 1, 1, 0, D)
             send_dproj(l - 1, 2, N - D, D)
-        smh[h, 3 * LAYERS + l : 3 * LAYERS + l + 1, :] = jnp.sum(g_sum, axis=0, keepdims=True)
+        sml[3 * LAYERS + l : 3 * LAYERS + l + 1, :] = jnp.sum(g_sum, axis=0, keepdims=True)
 
     c = pltpu.make_async_copy(tg_out, tg_hbm, osem.at[0])
     c.start()
     outs.append(c)
     if inside:
-        small = to_hap(lambda t: smh.at[h], lambda d: smh.at[h], lambda d: smhs.at[d], lambda d: smhr.at[d])
-        for l in range(1, LAYERS):
-            reduced(l)
+        def quarter(t):
+            return pl.ds(pl.multiple_of(t * Cq, Cq), Cq)
+
+        smh[h] = sml[:, quarter(h)]
+        small = to_hap(
+            lambda t: sml.at[:, quarter(t)], lambda d: smh.at[h], lambda d: smhs.at[d], lambda d: smhr.at[d])
+        forward(0)
         for c in small:
             c.wait_recv()
         total = smh[0]
@@ -369,6 +400,8 @@
             total = total + smh[q]
         sms[me] = total
         small = to_seq(lambda t: sms.at[me], lambda d: sms.at[me], lambda d: smss.at[d], lambda d: smsr.at[d])
+        for l in range(1, LAYERS):
+            reduced(l)
         reduced(0)
         for l in range(1, LAYERS):
             start_out(l)
@@ -377,15 +410,21 @@
         total = sms[0]
         for q in range(1, n):
             total = total + sms[q]
+        sma[h] = total
+        small = to_hap(lambda t: sma.at[h], lambda d: sma.at[h], lambda d: smas.at[d], lambda d: smar.at[d])
+        for c in small:
+            c.wait_recv()
+        parts = [(q * Cq, Cq, sma[q]) for q in range(haps)]
     else:
-        total = smh[h]
+        parts = [(0, C, sml[...])]
         for l in range(LAYERS):
             c = pltpu.make_async_copy(pg_out.at[l], pg_hbm.at[l], osem.at[3 + l])
             c.start()
             outs.append(c)
-    for j in range(3):
-        tp_out[j] = total[j * LAYERS : (j + 1) * LAYERS, :]
-    gn_out[...] = total[3 * LAYERS :, :]
+    for at, size, total in parts:
+        for j in range(3):
+            tp_out[j, :, at : at + size] = total[j * LAYERS : (j + 1) * LAYERS, :]
+        gn_out[:, at : at + size] = total[3 * LAYERS :, :]
     for c in (pltpu.make_async_copy(tp_out, tp_hbm, osem.at[1]), pltpu.make_async_copy(gn_out, gn_hbm, osem.at[2])):
         c.start()
         outs.append(c)
@@ -399,22 +438,25 @@
         c.wait()
 
 
-def finish(a, b, c, d, a_out, b_out, c_out, d_out, sem):
-    copies = [
-        pltpu.make_async_copy(x, y, sem.at[j])
-        for j, (x, y) in enumerate(((b, b_out), (a, a_out), (c, c_out), (d, d_out)))
-    ]
-    for x in copies:
+def finish(a, b, c, d, a_out, b_out, c_out, d_out, a_in, b_in, c_in, d_in, sem):
+    refs = ((b, b_in, b_out), (a, a_in, a_out), (c, c_in, c_out), (d, d_in, d_out))
+    loads = [pltpu.make_async_copy(x, y, sem.at[0, j]) for j, (x, y, _) in enumerate(refs)]
+    stores = [pltpu.make_async_copy(y, z, sem.at[1, j]) for j, (_, y, z) in enumerate(refs)]
+    for x in loads:
         x.start()
-    for x in copies:
+    for x, y in zip(loads, stores):
         x.wait()
+        y.start()
+    for y in stores:
+        y.wait()
 
 
 def shards(n, haps, tokens, cotangent, gaps, conv_taps, norm_gains, projection):
     x = tokens[0]
     N, C = x.shape
     PR = projection.shape[2]
-    inside = n > 1 and haps == 4 and C % (16 * n) == 0 and PR % (128 * haps) == 0
+    inside = n > 2 and n % 2 == 0 and haps == 4 and C % (16 * n) == 0 and C % (128 * haps) == 0
+    Cq, nz = C // haps, max(n // 2, 1)
     Q, rows = PR // haps, max(C // n, 1)
     L = LAYERS
     wide = haps if inside else 1
@@ -435,10 +477,11 @@
         pltpu.VMEM((L, N, PR), BF16), pltpu.VMEM((L, N + 2 * D, C), F32), pltpu.VMEM((N, C), F32),
         pltpu.VMEM((L, C, N * wide), BF16), dma(L, haps), dma(L, haps),
         opt((L, N * haps, Q), BF16), dma(L, haps, 3), dma(L, haps, 3),
-        opt((L, n, rows, Q), BF16), opt((L, n, rows, Q), BF16), dma(L, n), dma(L, n),
+        opt((L, n, rows, Q), BF16), opt((L, nz, rows, Q), BF16), dma(L, nz), dma(L, nz),
+        opt((L, rows, Q), F32), opt((L, nz, rows, Q), BF16), opt((L, nz, rows, Q), BF16), dma(L, nz), dma(L, nz),
         opt((L, haps, rows, Q), BF16), dma(L, haps), dma(L, haps),
-        pltpu.VMEM((haps, 4 * L, C), F32), dma(haps), dma(haps),
-        opt((n, 4 * L, C), F32), dma(n), dma(n),
+        pltpu.VMEM((4 * L, C), F32), opt((haps, 4 * L, Cq), F32), dma(haps), dma(haps),
+        opt((n, 4 * L, Cq), F32), dma(n), dma(n), opt((haps, 4 * L, Cq), F32), dma(haps), dma(haps),
     ]
     hbm = pl.BlockSpec(memory_space=pltpu.HBM)
     outs = [
@@ -460,7 +503,7 @@
             out_shape=outs,
             in_specs=[hbm] * 4,
             out_specs=[hbm] * 4,
-            scratch_shapes=[dma(4)],
+            scratch_shapes=[pltpu.VMEM(o.shape, o.dtype) for o in outs] + [dma(2, 4)],
             compiler_params=pltpu.CompilerParams(**params),
         )(tg, pg, taps, gains)
     else:

time: 62.6 us -> 43.1 us (0.69)
  Pallas kernels: 61.9 us -> 42.3 us
    pallas_call x1, Pallas kernels: 21.5 us -> 1.94 us  [shards(): pl.pallas_call(finish, out_shape=outs, in_specs=[hbm] * 4, out_specs=[hbm...]
where the time goes in v4:
time: 43.1 us; the launch traced here: 42.9 us
  Pallas kernels  42.3 us (98%)
  between operations  0.64 us (1%)
    pallas_call x1, Pallas kernels, shards(): pl.pallas_call(functools.partial(kernel, n, haps, inside), out_shape=outs...  40.3 us
    pallas_call x1, Pallas kernels, shards(): pl.pallas_call(finish, out_shape=outs, in_specs=[hbm] * 4, out_specs=[hbm...  1.94 us

profile of v4, /device:TPU:0, one launch (start us, length us, event | category | flops | bytes accessed | tf_op | source)
XLA Modules:
  0.0 42.9 jit_solution(5030316101524630711)
XLA Ops:
  0.6 40.3 %shard_map.93 = (bf16[128,512]{1,0:T(8,128)(2,1)}, f32[2,64,1024]{2,1,0:T(8,128)}, f32[3,2,512]{2,1,0:T(2,128)}, f32[2,512]{1,0:T(2,128)}) custom-call(bf16[128,512]{1,0:T(8,128)(2,1)} %bitcast.5, bf16[128,512]{1,0:T(8,128)(2,1)} %bitcast.6, s32[1,2]{1,0:T(1,128)} %gaps_hbm.1, f32[3,2,512]{2,1,0:T(2,128)} %bitcast.7, f32[2,512]{1,0:T(2,128)} %gains_hbm.1, ...), custom_call_target="tpu_custom_call" | custom-call | tf_op jit(solution)/shard_map/pallas_call | solution.py:492
  41.0 1.9 %shard_map.94 = (bf16[128,512]{1,0:T(8,128)(2,1)}, f32[2,64,1024]{2,1,0:T(8,128)}, f32[3,2,512]{2,1,0:T(2,128)}, f32[2,512]{1,0:T(2,128)}) custom-call(bf16[128,512]{1,0:T(8,128)(2,1)} %get-tuple-element.12.a, f32[2,64,1024]{2,1,0:T(8,128)} %get-tuple-element.13.b, f32[3,2,512]{2,1,0:T(2,128)} %get-tuple-element.14.c, f32[2,512]{1,0:T(2,128)} %get-tuple-element.15.d), custom_call_target="tpu_custom_call" | custom-call | tf_op jit(solution)/shard_map/pallas_call | solution.py:501

commit v5 on v4

--- a/solution.py
+++ b/solution.py
@@ -20,8 +20,8 @@
 def kernel(
     n, haps, inside,
     tok_hbm, cot_hbm, gaps_hbm, taps_hbm, gains_hbm, w_hbm,
-    tg_hbm, pg_hbm, tp_hbm, gn_hbm,
-    tg_out, pg_out, tp_out, gn_out, osem, tok, cot, gaps, taps, gains, isem, w, wsem, edge_out, halo_in, hs, hr, xs, inv, npad, dgelu, hid, proj, dp, dpad, gcur,
+    tg_hbm, pg_hbm, sm_hbm,
+    tg_out, pg_out, osem, tok, cot, gaps, taps, gains, isem, w, wsem, edge_out, halo_in, hs, hr, xs, inv, npad, dgelu, hid, proj, dp, dpad, gcur,
     hT, hTs, hTr, dq_in, dqs, dqr, gbf, xr, xrs, xrr, own, zb, zr, zrs, zrr, ag, ags, agr, sml, smh, smhs, smhr, sms, smss, smsr, sma, smas, smar,
 ):
     me, h = lax.axis_index("seq"), lax.axis_index("hap")
@@ -185,75 +185,121 @@
     hT_copies = [None] * LAYERS
 
     def send_hidden(l):
-        hT[l, :, 0:N] = jnp.transpose(hid[l].astype(F32)).astype(BF16)
+        hT[l, 0] = jnp.transpose(hid[l].astype(F32)).astype(BF16)
         if inside:
             hT_copies[l] = to_hap(
-                lambda t: hT.at[l, :, pl.ds(0, N)], lambda d: hT.at[l, :, pl.ds(d * N, N)],
+                lambda t: hT.at[l, 0], lambda d: hT.at[l, d],
                 lambda d: hTs.at[l, d], lambda d: hTr.at[l, d], (1, 2))
 
     def relay_hidden(l):
         if inside:
             hT_copies[l][1].wait_recv()
             hT_copies[l] = [hT_copies[l][0]] + to_hap(
-                lambda t: hT.at[l, :, pl.ds(2 * N, N)], lambda d: hT.at[l, :, pl.ds(d * N, N)],
+                lambda t: hT.at[l, 2], lambda d: hT.at[l, d],
                 lambda d: hTs.at[l, d], lambda d: hTr.at[l, d], (3,), 1)
 
-    def start_out(l):
-        for c in ag_copies[l]:
-            c.wait_recv()
-        for q in range(haps):
-            pg_out[l, :, q * Q : (q + 1) * Q] = ag[l, q].astype(F32)
-        c = pltpu.make_async_copy(pg_out.at[l], pg_hbm.at[l], osem.at[3 + l])
-        c.start()
-        outs.append(c)
-
-    outs = []
-    for l in range(LAYERS):
-        gain = gains[l : l + 1, :]
-        for i in range(chunks):
-            x = xs[l, ds(i), :].astype(F32)
-            r = rms(x)
-            inv[l, ds(i), :] = r
-            npad[l, ds(i + 1), :] = x * r * gain * valid[i]
-        for i in inner:
-            forward_chunk(l, i)
-        halo_wait(l)
-        for side, at in ((0, 0), (1, chunks + 1)):
-            x = halo_in[l, side].astype(F32)
-            npad[l, ds(at), :] = x * rms(x) * gain
-        for i in outer:
-            forward_chunk(l, i)
-        if l + 1 == LAYERS:
-            send_hidden(l)
-        loads[l].wait()
-        proj[l] = jnp.dot(hid[l], w[l], preferred_element_type=F32)
-        if l + 1 < LAYERS:
-            for i in outer + inner:
-                first = proj[l, ds(i), 0:C]
-                gate = 0.5 + 0.5 * jnp.tanh(0.5 * proj[l, ds(i), C:PR])
-                proj[l, ds(i), C:PR] = gate
+    def norm_chunk(l, i):
+        v = xs[l, ds(i), :].astype(F32)
+        r = rms(v)
+        inv[l, ds(i), :] = r
+        npad[l, ds(i + 1), :] = v * r * gains[l : l + 1, :] * valid[i]
+
+    def project(l, which):
+        y = jnp.dot(
+            jnp.concatenate([hid[l, ds(i), :] for i in which], axis=0), w[l], preferred_element_type=F32)
+        for j, i in enumerate(which):
+            first = y[j * D : (j + 1) * D, 0:C]
+            gate = 0.5 + 0.5 * jnp.tanh(0.5 * y[j * D : (j + 1) * D, C:PR])
+            proj[l, ds(i), 0:C] = first
+            proj[l, ds(i), C:PR] = gate
+            if l + 1 < LAYERS:
                 nxt = (xs[l, ds(i), :].astype(F32) + valid[i] * first * gate).astype(BF16)
                 xs[l + 1, ds(i), :] = nxt
                 if i in outer:
                     edge_out[l + 1, 0 if i == 0 else 1] = (nxt.astype(F32) * valid[i]).astype(BF16)
-                if i == outer[-1]:
-                    halo_start(l + 1)
-        if l + 1 < LAYERS:
-            send_hidden(l)
-
+
+    def dproj(l, i):
+        first = proj[l, ds(i), 0:C]
+        gate = proj[l, ds(i), C:PR]
+        grad = cot[ds(i), :].astype(F32) if l == LAYERS - 1 else gcur[ds(i), :]
+        bg = valid[i] * grad * gate
+        both = jnp.concatenate([bg, bg * first * (1.0 - gate)], axis=1).astype(BF16)
+        for q in range(haps):
+            dp[l, q, ds(i), :] = both[:, q * Q : (q + 1) * Q]
+
+    def send_dproj(l, which):
+        if not inside:
+            return
+        blocks = [(0, D, N - 2 * D)] if which == inner else [(1, 0, D), (2, N - D, D)]
+        for j, start, size in blocks:
+            dq_copies[l] += to_hap(
+                lambda t: dp.at[l, t, pl.ds(start, size), :],
+                lambda d: dq_in.at[l, pl.ds(d * N + start, size), :],
+                lambda d: dqs.at[l, d, j], lambda d: dqr.at[l, d, j])
+
+    def dconv(l, which):
+        y = lax.dot_general(
+            jnp.concatenate(
+                [jnp.concatenate([dp[l, q, ds(i), :] for q in range(haps)], axis=1) for i in which], axis=0),
+            w[l], (((1,), (1,)), ((), ())), preferred_element_type=F32)
+        for j, i in enumerate(which):
+            dpre = y[j * D : (j + 1) * D, :] * dgelu[l, ds(i), :]
+            dpad[l, ds(i + 1), :] = dpre
+            if i in outer:
+                edge_out[2 * LAYERS - 1 - l, 0 if i == 0 else 1] = dpre.astype(BF16)
+
+    def fold(v):
+        return jnp.sum(v.reshape(D // 8, 8, C), axis=0)
+
+    outs = []
     dq_copies, x_copies, z_copies, ag_copies = [[[] for _ in range(LAYERS)] for _ in range(4)]
     nz = n // 2
     z, x = me // 2, lax.rem(me, 2)
     order = [nz // 2] + [j for j in range(1, nz) if j != nz // 2] + [0]
 
+    for l in range(LAYERS):
+        last = l == LAYERS - 1
+        for i in range(chunks):
+            norm_chunk(l, i)
+        for i in inner:
+            forward_chunk(l, i)
+        loads[l].wait()
+        project(l, inner)
+        if last:
+            small_in[4].wait()
+            for i in inner:
+                dproj(l, i)
+            send_dproj(l, inner)
+            dconv(l, inner)
+        halo_wait(l)
+        for side, at in ((0, 0), (1, chunks + 1)):
+            v = halo_in[l, side].astype(F32)
+            npad[l, ds(at), :] = v * rms(v) * gains[l : l + 1, :]
+        for i in outer:
+            forward_chunk(l, i)
+        if last:
+            send_hidden(l)
+        project(l, outer)
+        if last:
+            for i in outer:
+                dproj(l, i)
+            dconv(l, outer)
+            halo_start(l + 1)
+            send_dproj(l, outer)
+        else:
+            halo_start(l + 1)
+            send_hidden(l)
+
     def gram(l):
         if not inside:
-            pg_out[l] = jnp.dot(hT[l], dp[l], preferred_element_type=F32)
+            pg_out[l] = jnp.dot(
+                hT[l, 0], jnp.concatenate([dp[l, q] for q in range(haps)], axis=1), preferred_element_type=F32)
             return
-        dq_in[l, 0:N, :] = dp[l, :, pl.ds(pl.multiple_of(h * Q, Q), Q)]
+        dq_in[l, 0:N, :] = dp[l, h]
         for c in hT_copies[l] + dq_copies[l]:
             c.wait_recv()
-        g = jnp.dot(hT[l], dq_in[l], preferred_element_type=F32)
+        g = jnp.dot(
+            jnp.concatenate([hT[l, d] for d in range(haps)], axis=1), dq_in[l], preferred_element_type=F32)
         gbf[l] = g.astype(BF16).reshape(n, rows, Q)
         for j in order:
             c = pltpu.make_async_remote_copy(
@@ -285,52 +331,18 @@
         for j, c in z_copies[l]:
             c.wait_recv()
             total = total + zr[l, j].astype(F32)
-        ag[l, h] = total.astype(BF16)
+        ag[l] = total.astype(BF16)
         ag_copies[l] = to_hap(
-            lambda t: ag.at[l, h], lambda d: ag.at[l, h], lambda d: ags.at[l, d], lambda d: agr.at[l, d])
-
-    def dproj(l, i):
-        last = l == LAYERS - 1
-        first = proj[l, ds(i), 0:C]
-        gate = proj[l, ds(i), C:PR]
-        if last:
-            gate = 0.5 + 0.5 * jnp.tanh(0.5 * gate)
-        grad = cot[ds(i), :].astype(F32) if last else gcur[ds(i), :]
-        bg = valid[i] * grad * gate
-        dp[l, ds(i), 0:C] = bg.astype(BF16)
-        dp[l, ds(i), C:PR] = (bg * first * (1.0 - gate)).astype(BF16)
-
-    def send_dproj(l, j, start, size):
-        if inside:
-            dq_copies[l] += to_hap(
-                lambda t: dp.at[l, pl.ds(start, size), pl.ds(pl.multiple_of(t * Q, Q), Q)],
-                lambda d: dq_in.at[l, pl.ds(d * N + start, size), :],
-                lambda d: dqs.at[l, d, j], lambda d: dqr.at[l, d, j])
-
-    def fold(x):
-        return jnp.sum(x.reshape(D // 8, 8, C), axis=0)
-
-    small_in[4].wait()
+            lambda t: ag.at[l], lambda d: pg_hbm.at[l, h], lambda d: ags.at[l, d], lambda d: agr.at[l, d])
+        c = pltpu.make_async_copy(ag.at[l], pg_hbm.at[l, h], osem.at[2 + l])
+        c.start()
+        outs.append(c)
+
     for l in range(LAYERS - 1):
         relay_hidden(l)
-    for i in range(chunks):
-        dproj(LAYERS - 1, i)
-    send_dproj(LAYERS - 1, 0, 0, N)
     for l in reversed(range(LAYERS)):
         k = 2 * LAYERS - 1 - l
         last = l == LAYERS - 1
-        gain = gains[l : l + 1, :]
-        if not last:
-            gram(l + 1)
-        dpad[l, pl.ds(D, N), :] = lax.dot_general(
-            dp[l], w[l], (((1,), (1,)), ((), ())), preferred_element_type=F32)
-        for i in outer + inner:
-            dpre = dpad[l, ds(i + 1), :] * dgelu[l, ds(i), :]
-            dpad[l, ds(i + 1), :] = dpre
-            if i in outer:
-                edge_out[k, 0 if i == 0 else 1] = dpre.astype(BF16)
-            if i == outer[-1]:
-                halo_start(k)
         g_sum = jnp.zeros((8, C), F32)
 
         def back_chunk(i, g_sum):
@@ -340,13 +352,13 @@
                 + taps[2, l : l + 1, :] * dpad[l, ds(i), :]
             )
             dq = dn * valid[i]
-            x = xs[l, ds(i), :].astype(F32)
+            v = xs[l, ds(i), :].astype(F32)
             r = inv[l, ds(i), :]
-            xr = x * r
-            g_sum = g_sum + fold(dq * xr)
-            dt = dq * gain
+            vr = v * r
+            g_sum = g_sum + fold(dq * vr)
+            dt = dq * gains[l : l + 1, :]
             grad = cot[ds(i), :].astype(F32) if last else gcur[ds(i), :]
-            new = grad + r * dt - xr * (r * r * jnp.mean(dt * x, axis=-1, keepdims=True))
+            new = grad + r * dt - vr * (r * r * jnp.mean(dt * v, axis=-1, keepdims=True))
             if l == 0:
                 tg_out[ds(i), :] = new.astype(BF16)
             else:
@@ -357,7 +369,8 @@
         for i in inner:
             g_sum = back_chunk(i, g_sum)
         if l > 0:
-            send_dproj(l - 1, 0, D, N - 2 * D)
+            send_dproj(l - 1, inner)
+            dconv(l - 1, inner)
         t_sum = [jnp.zeros((8, C), F32) for _ in range(3)]
         for i in range(chunks):
             dpre = dpad[l, ds(i + 1), :]
@@ -371,15 +384,16 @@
                     forward(m)
             gram(0)
         halo_wait(k)
-        if last:
-            relay_hidden(l)
         dpad[l, ds(0), :] = halo_in[k, 0].astype(F32)
         dpad[l, ds(chunks + 1), :] = halo_in[k, 1].astype(F32)
         for i in outer:
             g_sum = back_chunk(i, g_sum)
         if l > 0:
-            send_dproj(l - 1, 1, 0, D)
-            send_dproj(l - 1, 2, N - D, D)
+            send_dproj(l - 1, outer)
+            relay_hidden(l)
+            dconv(l - 1, outer)
+            halo_start(k + 1)
+            gram(l)
         sml[3 * LAYERS + l : 3 * LAYERS + l + 1, :] = jnp.sum(g_sum, axis=0, keepdims=True)
 
     c = pltpu.make_async_copy(tg_out, tg_hbm, osem.at[0])
@@ -403,33 +417,28 @@
         for l in range(1, LAYERS):
             reduced(l)
         reduced(0)
-        for l in range(1, LAYERS):
-            start_out(l)
         for c in small:
             c.wait_recv()
         total = sms[0]
         for q in range(1, n):
             total = total + sms[q]
-        sma[h] = total
-        small = to_hap(lambda t: sma.at[h], lambda d: sma.at[h], lambda d: smas.at[d], lambda d: smar.at[d])
+        sma[...] = total
+        small = to_hap(lambda t: sma, lambda d: sm_hbm.at[h], lambda d: smas.at[d], lambda d: smar.at[d])
+        c = pltpu.make_async_copy(sma, sm_hbm.at[h], osem.at[1])
+        c.start()
+        outs.append(c)
+        for l in reversed(range(LAYERS)):
+            small += ag_copies[l]
         for c in small:
             c.wait_recv()
-        parts = [(q * Cq, Cq, sma[q]) for q in range(haps)]
     else:
-        parts = [(0, C, sml[...])]
+        c = pltpu.make_async_copy(sml, sm_hbm.at[0], osem.at[1])
+        c.start()
+        outs.append(c)
         for l in range(LAYERS):
-            c = pltpu.make_async_copy(pg_out.at[l], pg_hbm.at[l], osem.at[3 + l])
+            c = pltpu.make_async_copy(pg_out.at[l], pg_hbm.at[l], osem.at[2 + l])
             c.start()
             outs.append(c)
-    for at, size, total in parts:
-        for j in range(3):
-            tp_out[j, :, at : at + size] = total[j * LAYERS : (j + 1) * LAYERS, :]
-        gn_out[:, at : at + size] = total[3 * LAYERS :, :]
-    for c in (pltpu.make_async_copy(tp_out, tp_hbm, osem.at[1]), pltpu.make_async_copy(gn_out, gn_hbm, osem.at[2])):
-        c.start()
-        outs.append(c)
-    if inside:
-        start_out(0)
     for k in range(2 * LAYERS):
         halo_drain(k)
     for c in sends:
@@ -438,17 +447,32 @@
         c.wait()
 
 
-def finish(a, b, c, d, a_out, b_out, c_out, d_out, a_in, b_in, c_in, d_in, sem):
-    refs = ((b, b_in, b_out), (a, a_in, a_out), (c, c_in, c_out), (d, d_in, d_out))
-    loads = [pltpu.make_async_copy(x, y, sem.at[0, j]) for j, (x, y, _) in enumerate(refs)]
-    stores = [pltpu.make_async_copy(y, z, sem.at[1, j]) for j, (_, y, z) in enumerate(refs)]
-    for x in loads:
-        x.start()
-    for x, y in zip(loads, stores):
-        x.wait()
-        y.start()
-    for y in stores:
-        y.wait()
+def finish(tg, pg, sm, tg_hbm, pg_hbm, tp_hbm, gn_hbm, tg_v, pg_in, sm_in, pg_v, tp_v, gn_v, sem):
+    L, haps, _, Q = pg.shape
+    Cq = sm.shape[2]
+    loads = [
+        pltpu.make_async_copy(a, b, sem.at[0, j]) for j, (a, b) in enumerate(((pg, pg_in), (tg, tg_v), (sm, sm_in)))]
+    stores = [
+        pltpu.make_async_copy(a, b, sem.at[1, j])
+        for j, (a, b) in enumerate(((pg_v, pg_hbm), (tg_v, tg_hbm), (tp_v, tp_hbm), (gn_v, gn_hbm)))]
+    for c in loads:
+        c.start()
+    loads[0].wait()
+    for l in range(L):
+        for q in range(haps):
+            pg_v[l, :, q * Q : (q + 1) * Q] = pg_in[l, q].astype(F32)
+    stores[0].start()
+    loads[1].wait()
+    stores[1].start()
+    loads[2].wait()
+    for q in range(haps):
+        for j in range(3):
+            tp_v[j, :, q * Cq : (q + 1) * Cq] = sm_in[q, j * L : (j + 1) * L, :]
+        gn_v[:, q * Cq : (q + 1) * Cq] = sm_in[q, 3 * L :, :]
+    stores[2].start()
+    stores[3].start()
+    for c in stores:
+        c.wait()
 
 
 def shards(n, haps, tokens, cotangent, gaps, conv_taps, norm_gains, projection):
@@ -474,41 +498,48 @@
         pltpu.VMEM((2 * L, 2, D, C), BF16), pltpu.VMEM((2 * L, 2, D, C), BF16), dma(2 * L, 2), dma(2 * L, 2),
         pltpu.VMEM((L, N, C), BF16), pltpu.VMEM((L, N, 1), F32), pltpu.VMEM((L, N + 2 * D, C), F32),
         pltpu.VMEM((L, N, C), F32), pltpu.VMEM((L, N, C), BF16), pltpu.VMEM((L, N, PR), F32),
-        pltpu.VMEM((L, N, PR), BF16), pltpu.VMEM((L, N + 2 * D, C), F32), pltpu.VMEM((N, C), F32),
-        pltpu.VMEM((L, C, N * wide), BF16), dma(L, haps), dma(L, haps),
+        pltpu.VMEM((L, haps, N, Q), BF16), pltpu.VMEM((L, N + 2 * D, C), F32), pltpu.VMEM((N, C), F32),
+        pltpu.VMEM((L, wide, C, N), BF16), dma(L, haps), dma(L, haps),
         opt((L, N * haps, Q), BF16), dma(L, haps, 3), dma(L, haps, 3),
         opt((L, n, rows, Q), BF16), opt((L, nz, rows, Q), BF16), dma(L, nz), dma(L, nz),
         opt((L, rows, Q), F32), opt((L, nz, rows, Q), BF16), opt((L, nz, rows, Q), BF16), dma(L, nz), dma(L, nz),
-        opt((L, haps, rows, Q), BF16), dma(L, haps), dma(L, haps),
+        opt((L, rows, Q), BF16), dma(L, haps), dma(L, haps),
         pltpu.VMEM((4 * L, C), F32), opt((haps, 4 * L, Cq), F32), dma(haps), dma(haps),
-        opt((n, 4 * L, Cq), F32), dma(n), dma(n), opt((haps, 4 * L, Cq), F32), dma(haps), dma(haps),
+        opt((n, 4 * L, Cq), F32), dma(n), dma(n), opt((4 * L, Cq), F32), dma(haps), dma(haps),
     ]
     hbm = pl.BlockSpec(memory_space=pltpu.HBM)
+    tg_shape = jax.ShapeDtypeStruct((N, C), BF16)
     outs = [
-        jax.ShapeDtypeStruct((N, C), BF16), jax.ShapeDtypeStruct((L, rows if inside else C, PR), F32),
-        jax.ShapeDtypeStruct((3, L, C), F32), jax.ShapeDtypeStruct((L, C), F32)]
-    scratch = [pltpu.VMEM(o.shape, o.dtype) for o in outs] + [dma(3 + L)] + scratch
+        tg_shape,
+        jax.ShapeDtypeStruct((L, haps, rows, Q), BF16) if inside else jax.ShapeDtypeStruct((L, C, PR), F32),
+        jax.ShapeDtypeStruct((haps, 4 * L, Cq) if inside else (1, 4 * L, C), F32)]
+    scratch = [
+        pltpu.VMEM((N, C), BF16), pltpu.VMEM((16, 128) if inside else (L, C, PR), F32), dma(2 + L)] + scratch
     params = dict(vmem_limit_bytes=60 * 1024 * 1024)
-    tg, pg, taps, gains = pl.pallas_call(
+    tg, pg, sm = pl.pallas_call(
         functools.partial(kernel, n, haps, inside),
         out_shape=outs,
         in_specs=[hbm] * 6,
-        out_specs=[hbm] * 4,
+        out_specs=[hbm] * 3,
         scratch_shapes=scratch,
         compiler_params=pltpu.CompilerParams(collective_id=0, has_side_effects=True, **params),
     )(x, cotangent[0], gaps, jnp.transpose(conv_taps, (1, 0, 2)), norm_gains, projection)
     if inside:
+        finals = [
+            tg_shape, jax.ShapeDtypeStruct((L, rows, PR), F32),
+            jax.ShapeDtypeStruct((3, L, C), F32), jax.ShapeDtypeStruct((L, C), F32)]
         tg, pg, taps, gains = pl.pallas_call(
             finish,
-            out_shape=outs,
-            in_specs=[hbm] * 4,
+            out_shape=finals,
+            in_specs=[hbm] * 3,
             out_specs=[hbm] * 4,
-            scratch_shapes=[pltpu.VMEM(o.shape, o.dtype) for o in outs] + [dma(2, 4)],
+            scratch_shapes=[pltpu.VMEM(o.shape, o.dtype) for o in outs + finals[1:]] + [dma(2, 4)],
             compiler_params=pltpu.CompilerParams(**params),
-        )(tg, pg, taps, gains)
+        )(tg, pg, sm)
     else:
         pg = lax.psum(lax.psum_scatter(pg, "seq", scatter_dimension=1, tiled=True), "hap")
-        taps, gains = lax.psum((taps, gains), ("seq", "hap"))
+        sm = lax.psum(sm[0], ("seq", "hap"))
+        taps, gains = sm[: 3 * L].reshape(3, L, C), sm[3 * L :]
     return tg[None], pg, jnp.transpose(taps, (1, 0, 2)), gains
 
 

time: 43.1 us -> 41.1 us (0.954)
  Pallas kernels: 42.3 us -> 40.3 us
    pallas_call x1, Pallas kernels: 40.3 us -> 38.4 us  [shards(): pl.pallas_call(functools.partial(kernel, n, haps, inside), out_shape=outs...]
where the time goes in v5:
time: 41.1 us; the launch traced here: 41 us
  Pallas kernels  40.3 us (98%)
  between operations  0.64 us (2%)
    pallas_call x1, Pallas kernels, shards(): pl.pallas_call(functools.partial(kernel, n, haps, inside), out_shape=outs...  38.4 us
    pallas_call x1, Pallas kernels, shards(): pl.pallas_call(finish, out_shape=finals, in_specs=[hbm] * 3, out_specs=[h...  1.89 us

profile of v5, /device:TPU:0, one launch (start us, length us, event | category | flops | bytes accessed | tf_op | source)
XLA Modules:
  0.0 41.0 jit_solution(3512470660834772684)
XLA Ops:
  0.6 38.4 %shard_map.93 = (bf16[128,512]{1,0:T(8,128)(2,1)}, bf16[2,4,64,256]{3,2,1,0:T(8,128)(2,1)}, f32[4,8,128]{2,1,0:T(8,128)}) custom-call(bf16[128,512]{1,0:T(8,128)(2,1)} %bitcast.5, bf16[128,512]{1,0:T(8,128)(2,1)} %bitcast.6, s32[1,2]{1,0:T(1,128)} %gaps_hbm.1, f32[3,2,512]{2,1,0:T(2,128)} %bitcast.7, f32[2,512]{1,0:T(2,128)} %gains_hbm.1, ...), custom_call_target="tpu_custom_call" | custom-call | tf_op jit(solution)/shard_map/pallas_call | solution.py:519
  39.1 1.9 %shard_map.94 = (bf16[128,512]{1,0:T(8,128)(2,1)}, f32[2,64,1024]{2,1,0:T(8,128)}, f32[3,2,512]{2,1,0:T(2,128)}, f32[2,512]{1,0:T(2,128)}) custom-call(bf16[128,512]{1,0:T(8,128)(2,1)} %get-tuple-element.11.tg, bf16[2,4,64,256]{3,2,1,0:T(8,128)(2,1)} %get-tuple-element.12.pg, f32[4,8,128]{2,1,0:T(8,128)} %get-tuple-element.13.sm), custom_call_target="tpu_custom_call" | custom-call | tf_op jit(solution)/shard_map/pallas_call | solution.py:531

commit v6 on v5

--- a/solution.py
+++ b/solution.py
@@ -179,24 +179,39 @@
         th = jnp.tanh(GELU_C * (pre + GELU_A * (sq * pre)))
         half = 0.5 * (1.0 + th)
         hidden = (pre * half).astype(BF16)
-        hid[l, ds(i), :] = hidden
+        hid[l, 0, ds(i), :] = hidden
         dgelu[l, ds(i), :] = half + 0.5 * pre * (1.0 - th * th) * (GELU_C * (1.0 + 3.0 * GELU_A * sq))
 
-    hT_copies = [None] * LAYERS
-
-    def send_hidden(l):
-        hT[l, 0] = jnp.transpose(hid[l].astype(F32)).astype(BF16)
-        if inside:
-            hT_copies[l] = to_hap(
-                lambda t: hT.at[l, 0], lambda d: hT.at[l, d],
-                lambda d: hTs.at[l, d], lambda d: hTr.at[l, d], (1, 2))
+    hid_copies = [[[] for _ in range(4)] for _ in range(LAYERS)]
+
+    def blocks_of(which):
+        return [(0, D, N - 2 * D)] if which == inner else [(1, 0, D), (2, N - D, D)]
+
+    def send_hidden(l, which):
+        if not inside:
+            return
+        for j, start, size in blocks_of(which):
+            near, far = to_hap(
+                lambda t: hid.at[l, 0, pl.ds(start, size), :], lambda d: hid.at[l, d, pl.ds(start, size), :],
+                lambda d: hTs.at[l, d, j], lambda d: hTr.at[l, d, j], (1, 2))
+            hid_copies[l][1].append(near)
+            hid_copies[l][2].append(far)
 
     def relay_hidden(l):
         if inside:
-            hT_copies[l][1].wait_recv()
-            hT_copies[l] = [hT_copies[l][0]] + to_hap(
-                lambda t: hT.at[l, 2], lambda d: hT.at[l, d],
-                lambda d: hTs.at[l, d], lambda d: hTr.at[l, d], (3,), 1)
+            for c in hid_copies[l][2]:
+                c.wait_recv()
+            hid_copies[l][2] = []
+            hid_copies[l][3] = to_hap(
+                lambda t: hid.at[l, 2], lambda d: hid.at[l, d],
+                lambda d: hTs.at[l, d, 0], lambda d: hTr.at[l, d, 0], (3,), 1)
+
+    def turn(l, which):
+        for d in which:
+            if d == 0 or inside:
+                for c in hid_copies[l][d]:
+                    c.wait_recv()
+                hT[l, d] = jnp.transpose(hid[l, d].astype(F32)).astype(BF16)
 
     def norm_chunk(l, i):
         v = xs[l, ds(i), :].astype(F32)
@@ -206,7 +221,7 @@
 
     def project(l, which):
         y = jnp.dot(
-            jnp.concatenate([hid[l, ds(i), :] for i in which], axis=0), w[l], preferred_element_type=F32)
+            jnp.concatenate([hid[l, 0, ds(i), :] for i in which], axis=0), w[l], preferred_element_type=F32)
         for j, i in enumerate(which):
             first = y[j * D : (j + 1) * D, 0:C]
             gate = 0.5 + 0.5 * jnp.tanh(0.5 * y[j * D : (j + 1) * D, C:PR])
@@ -230,8 +245,7 @@
     def send_dproj(l, which):
         if not inside:
             return
-        blocks = [(0, D, N - 2 * D)] if which == inner else [(1, 0, D), (2, N - D, D)]
-        for j, start, size in blocks:
+        for j, start, size in blocks_of(which):
             dq_copies[l] += to_hap(
                 lambda t: dp.at[l, t, pl.ds(start, size), :],
                 lambda d: dq_in.at[l, pl.ds(d * N + start, size), :],
@@ -263,6 +277,7 @@
             norm_chunk(l, i)
         for i in inner:
             forward_chunk(l, i)
+        send_hidden(l, inner)
         loads[l].wait()
         project(l, inner)
         if last:
@@ -277,18 +292,15 @@
             npad[l, ds(at), :] = v * rms(v) * gains[l : l + 1, :]
         for i in outer:
             forward_chunk(l, i)
-        if last:
-            send_hidden(l)
         project(l, outer)
         if last:
             for i in outer:
                 dproj(l, i)
             dconv(l, outer)
-            halo_start(l + 1)
+        halo_start(l + 1)
+        send_hidden(l, outer)
+        if last:
             send_dproj(l, outer)
-        else:
-            halo_start(l + 1)
-            send_hidden(l)
 
     def gram(l):
         if not inside:
@@ -296,7 +308,7 @@
                 hT[l, 0], jnp.concatenate([dp[l, q] for q in range(haps)], axis=1), preferred_element_type=F32)
             return
         dq_in[l, 0:N, :] = dp[l, h]
-        for c in hT_copies[l] + dq_copies[l]:
+        for c in dq_copies[l]:
             c.wait_recv()
         g = jnp.dot(
             jnp.concatenate([hT[l, d] for d in range(haps)], axis=1), dq_in[l], preferred_element_type=F32)
@@ -338,8 +350,6 @@
         c.start()
         outs.append(c)
 
-    for l in range(LAYERS - 1):
-        relay_hidden(l)
     for l in reversed(range(LAYERS)):
         k = 2 * LAYERS - 1 - l
         last = l == LAYERS - 1
@@ -370,7 +380,11 @@
             g_sum = back_chunk(i, g_sum)
         if l > 0:
             send_dproj(l - 1, inner)
+            relay_hidden(l - 1)
             dconv(l - 1, inner)
+            turn(l - 1, (0, 1, 2))
+            if last:
+                turn(l, (0,))
         t_sum = [jnp.zeros((8, C), F32) for _ in range(3)]
         for i in range(chunks):
             dpre = dpad[l, ds(i + 1), :]
@@ -379,10 +393,11 @@
         for j in range(3):
             sml[LAYERS * j + l : LAYERS * j + l + 1, :] = jnp.sum(t_sum[j], axis=0, keepdims=True)
         if l == 0:
+            turn(0, (3,))
+            gram(0)
             if inside:
                 for m in range(1, LAYERS):
                     forward(m)
-            gram(0)
         halo_wait(k)
         dpad[l, ds(0), :] = halo_in[k, 0].astype(F32)
         dpad[l, ds(chunks + 1), :] = halo_in[k, 1].astype(F32)
@@ -390,9 +405,12 @@
             g_sum = back_chunk(i, g_sum)
         if l > 0:
             send_dproj(l - 1, outer)
-            relay_hidden(l)
             dconv(l - 1, outer)
             halo_start(k + 1)
+            if last:
+                relay_hidden(l)
+                turn(l, (1, 2))
+            turn(l, (3,))
             gram(l)
         sml[3 * LAYERS + l : 3 * LAYERS + l + 1, :] = jnp.sum(g_sum, axis=0, keepdims=True)
 
@@ -497,9 +515,9 @@
         pltpu.VMEM((L, C, PR), BF16), dma(L),
         pltpu.VMEM((2 * L, 2, D, C), BF16), pltpu.VMEM((2 * L, 2, D, C), BF16), dma(2 * L, 2), dma(2 * L, 2),
         pltpu.VMEM((L, N, C), BF16), pltpu.VMEM((L, N, 1), F32), pltpu.VMEM((L, N + 2 * D, C), F32),
-        pltpu.VMEM((L, N, C), F32), pltpu.VMEM((L, N, C), BF16), pltpu.VMEM((L, N, PR), F32),
+        pltpu.VMEM((L, N, C), F32), pltpu.VMEM((L, wide, N, C), BF16), pltpu.VMEM((L, N, PR), F32),
         pltpu.VMEM((L, haps, N, Q), BF16), pltpu.VMEM((L, N + 2 * D, C), F32), pltpu.VMEM((N, C), F32),
-        pltpu.VMEM((L, wide, C, N), BF16), dma(L, haps), dma(L, haps),
+        pltpu.VMEM((L, wide, C, N), BF16), dma(L, haps, 3), dma(L, haps, 3),
         opt((L, N * haps, Q), BF16), dma(L, haps, 3), dma(L, haps, 3),
         opt((L, n, rows, Q), BF16), opt((L, nz, rows, Q), BF16), dma(L, nz), dma(L, nz),
         opt((L, rows, Q), F32), opt((L, nz, rows, Q), BF16), opt((L, nz, rows, Q), BF16), dma(L, nz), dma(L, nz),

time: 41.1 us -> 39 us (0.949)
  Pallas kernels: 40.3 us -> 38.2 us
    pallas_call x1, Pallas kernels: 38.4 us -> 36.3 us  [shards(): pl.pallas_call(functools.partial(kernel, n, haps, inside), out_shape=outs...]
where the time goes in v6:
time: 39 us; the launch traced here: 38.9 us
  Pallas kernels  38.2 us (98%)
  between operations  0.64 us (2%)
    pallas_call x1, Pallas kernels, shards(): pl.pallas_call(functools.partial(kernel, n, haps, inside), out_shape=outs...  36.3 us
    pallas_call x1, Pallas kernels, shards(): pl.pallas_call(finish, out_shape=finals, in_specs=[hbm] * 3, out_specs=[h...  1.89 us

profile of v6, /device:TPU:0, one launch (start us, length us, event | category | flops | bytes accessed | tf_op | source)
XLA Modules:
  0.0 38.9 jit_solution(1624686662464042172)
XLA Ops:
  0.6 36.3 %shard_map.93 = (bf16[128,512]{1,0:T(8,128)(2,1)}, bf16[2,4,64,256]{3,2,1,0:T(8,128)(2,1)}, f32[4,8,128]{2,1,0:T(8,128)}) custom-call(bf16[128,512]{1,0:T(8,128)(2,1)} %bitcast.5, bf16[128,512]{1,0:T(8,128)(2,1)} %bitcast.6, s32[1,2]{1,0:T(1,128)} %gaps_hbm.1, f32[3,2,512]{2,1,0:T(2,128)} %bitcast.7, f32[2,512]{1,0:T(2,128)} %gains_hbm.1, ...), custom_call_target="tpu_custom_call" | custom-call | tf_op jit(solution)/shard_map/pallas_call | solution.py:537
  37.0 1.9 %shard_map.94 = (bf16[128,512]{1,0:T(8,128)(2,1)}, f32[2,64,1024]{2,1,0:T(8,128)}, f32[3,2,512]{2,1,0:T(2,128)}, f32[2,512]{1,0:T(2,128)}) custom-call(bf16[128,512]{1,0:T(8,128)(2,1)} %get-tuple-element.11.tg, bf16[2,4,64,256]{3,2,1,0:T(8,128)(2,1)} %get-tuple-element.12.pg, f32[4,8,128]{2,1,0:T(8,128)} %get-tuple-element.13.sm), custom_call_target="tpu_custom_call" | custom-call | tf_op jit(solution)/shard_map/pallas_call | solution.py:549

commit v7 on v6

--- a/solution.py
+++ b/solution.py
@@ -310,12 +310,15 @@
         dq_in[l, 0:N, :] = dp[l, h]
         for c in dq_copies[l]:
             c.wait_recv()
-        g = jnp.dot(
-            jnp.concatenate([hT[l, d] for d in range(haps)], axis=1), dq_in[l], preferred_element_type=F32)
-        gbf[l] = g.astype(BF16).reshape(n, rows, Q)
         for j in order:
+            t = lax.rem(z + j, nz)
+            cut = pl.ds(pl.multiple_of(t * 2 * rows, 2 * rows), 2 * rows)
+            g = jnp.dot(
+                jnp.concatenate([hT[l, d, cut, :] for d in range(haps)], axis=1), dq_in[l],
+                preferred_element_type=F32)
+            gbf[l, pl.ds(2 * t, 2)] = g.astype(BF16).reshape(2, rows, Q)
             c = pltpu.make_async_remote_copy(
-                src_ref=gbf.at[l, 2 * lax.rem(z + j, nz) + 1 - x], dst_ref=xr.at[l, j],
+                src_ref=gbf.at[l, 2 * t + 1 - x], dst_ref=xr.at[l, j],
                 send_sem=xrs.at[l, j], recv_sem=xrr.at[l, j],
                 device_id={"seq": 2 * z + 1 - x}, device_id_type=MESH)
             c.start()
@@ -349,6 +352,15 @@
         c = pltpu.make_async_copy(ag.at[l], pg_hbm.at[l, h], osem.at[2 + l])
         c.start()
         outs.append(c)
+
+    def tap_sums(l):
+        t_sum = [jnp.zeros((8, C), F32) for _ in range(3)]
+        for i in range(chunks):
+            dpre = dpad[l, ds(i + 1), :]
+            for j in range(3):
+                t_sum[j] = t_sum[j] + fold(dpre * npad[l, ds(i + j), :])
+        for j in range(3):
+            sml[LAYERS * j + l : LAYERS * j + l + 1, :] = jnp.sum(t_sum[j], axis=0, keepdims=True)
 
     for l in reversed(range(LAYERS)):
         k = 2 * LAYERS - 1 - l
@@ -376,6 +388,11 @@
                 dproj(l - 1, i)
             return g_sum
 
+        if l == 0:
+            turn(0, (3,))
+            gram(0)
+            for m in range(LAYERS):
+                tap_sums(m)
         for i in inner:
             g_sum = back_chunk(i, g_sum)
         if l > 0:
@@ -385,16 +402,7 @@
             turn(l - 1, (0, 1, 2))
             if last:
                 turn(l, (0,))
-        t_sum = [jnp.zeros((8, C), F32) for _ in range(3)]
-        for i in range(chunks):
-            dpre = dpad[l, ds(i + 1), :]
-            for j in range(3):
-                t_sum[j] = t_sum[j] + fold(dpre * npad[l, ds(i + j), :])
-        for j in range(3):
-            sml[LAYERS * j + l : LAYERS * j + l + 1, :] = jnp.sum(t_sum[j], axis=0, keepdims=True)
         if l == 0:
-            turn(0, (3,))
-            gram(0)
             if inside:
                 for m in range(1, LAYERS):
                     forward(m)

time: 39 us -> 38.8 us (level)
  no operation moved by 1% of the time
where the time goes in v7:
time: 38.8 us; the launch traced here: 38.6 us
  Pallas kernels  38 us (98%)
  between operations  0.64 us (2%)
    pallas_call x1, Pallas kernels, shards(): pl.pallas_call(functools.partial(kernel, n, haps, inside), out_shape=outs...  36.1 us
    pallas_call x1, Pallas kernels, shards(): pl.pallas_call(finish, out_shape=finals, in_specs=[hbm] * 3, out_specs=[h...  1.89 us

profile of v7, /device:TPU:0, one launch (start us, length us, event | category | flops | bytes accessed | tf_op | source)
XLA Modules:
  0.0 38.6 jit_solution(14189592497138069725)
XLA Ops:
  0.6 36.1 %shard_map.93 = (bf16[128,512]{1,0:T(8,128)(2,1)}, bf16[2,4,64,256]{3,2,1,0:T(8,128)(2,1)}, f32[4,8,128]{2,1,0:T(8,128)}) custom-call(bf16[128,512]{1,0:T(8,128)(2,1)} %bitcast.5, bf16[128,512]{1,0:T(8,128)(2,1)} %bitcast.6, s32[1,2]{1,0:T(1,128)} %gaps_hbm.1, f32[3,2,512]{2,1,0:T(2,128)} %bitcast.7, f32[2,512]{1,0:T(2,128)} %gains_hbm.1, ...), custom_call_target="tpu_custom_call" | custom-call | tf_op jit(solution)/shard_map/pallas_call | solution.py:545
  36.8 1.9 %shard_map.94 = (bf16[128,512]{1,0:T(8,128)(2,1)}, f32[2,64,1024]{2,1,0:T(8,128)}, f32[3,2,512]{2,1,0:T(2,128)}, f32[2,512]{1,0:T(2,128)}) custom-call(bf16[128,512]{1,0:T(8,128)(2,1)} %get-tuple-element.11.tg, bf16[2,4,64,256]{3,2,1,0:T(8,128)(2,1)} %get-tuple-element.12.pg, f32[4,8,128]{2,1,0:T(8,128)} %get-tuple-element.13.sm), custom_call_target="tpu_custom_call" | custom-call | tf_op jit(solution)/shard_map/pallas_call | solution.py:557

commit v8 on v7

--- a/solution.py
+++ b/solution.py
@@ -72,6 +72,9 @@
     def ds(i):
         return pl.ds(i * D, D)
 
+    def at(i):
+        return ds((outer + inner).index(i))
+
     def halo(k):
         up = pltpu.make_async_remote_copy(
             src_ref=edge_out.at[k, 1], dst_ref=halo_in.at[k, 0], send_sem=hs.at[k, 1],
@@ -179,13 +182,13 @@
         th = jnp.tanh(GELU_C * (pre + GELU_A * (sq * pre)))
         half = 0.5 * (1.0 + th)
         hidden = (pre * half).astype(BF16)
-        hid[l, 0, ds(i), :] = hidden
+        hid[l, 0, at(i), :] = hidden
         dgelu[l, ds(i), :] = half + 0.5 * pre * (1.0 - th * th) * (GELU_C * (1.0 + 3.0 * GELU_A * sq))
 
     hid_copies = [[[] for _ in range(4)] for _ in range(LAYERS)]
 
     def blocks_of(which):
-        return [(0, D, N - 2 * D)] if which == inner else [(1, 0, D), (2, N - D, D)]
+        return [(0, 2 * D, N - 2 * D)] if which == inner else [(1, 0, 2 * D)]
 
     def send_hidden(l, which):
         if not inside:
@@ -221,7 +224,7 @@
 
     def project(l, which):
         y = jnp.dot(
-            jnp.concatenate([hid[l, 0, ds(i), :] for i in which], axis=0), w[l], preferred_element_type=F32)
+            jnp.concatenate([hid[l, 0, at(i), :] for i in which], axis=0), w[l], preferred_element_type=F32)
         for j, i in enumerate(which):
             first = y[j * D : (j + 1) * D, 0:C]
             gate = 0.5 + 0.5 * jnp.tanh(0.5 * y[j * D : (j + 1) * D, C:PR])
@@ -240,7 +243,7 @@
         bg = valid[i] * grad * gate
         both = jnp.concatenate([bg, bg * first * (1.0 - gate)], axis=1).astype(BF16)
         for q in range(haps):
-            dp[l, q, ds(i), :] = both[:, q * Q : (q + 1) * Q]
+            dp[l, q, at(i), :] = both[:, q * Q : (q + 1) * Q]
 
     def send_dproj(l, which):
         if not inside:
@@ -254,7 +257,7 @@
     def dconv(l, which):
         y = lax.dot_general(
             jnp.concatenate(
-                [jnp.concatenate([dp[l, q, ds(i), :] for q in range(haps)], axis=1) for i in which], axis=0),
+                [jnp.concatenate([dp[l, q, at(i), :] for q in range(haps)], axis=1) for i in which], axis=0),
             w[l], (((1,), (1,)), ((), ())), preferred_element_type=F32)
         for j, i in enumerate(which):
             dpre = y[j * D : (j + 1) * D, :] * dgelu[l, ds(i), :]
@@ -287,9 +290,9 @@
             send_dproj(l, inner)
             dconv(l, inner)
         halo_wait(l)
-        for side, at in ((0, 0), (1, chunks + 1)):
+        for side, place in ((0, 0), (1, chunks + 1)):
             v = halo_in[l, side].astype(F32)
-            npad[l, ds(at), :] = v * rms(v) * gains[l : l + 1, :]
+            npad[l, ds(place), :] = v * rms(v) * gains[l : l + 1, :]
         for i in outer:
             forward_chunk(l, i)
         project(l, outer)

time: 38.8 us -> 38.8 us (level)
  no operation moved by 1% of the time
where the time goes in v8:
time: 38.8 us; the launch traced here: 38.6 us
  Pallas kernels  38 us (98%)
  between operations  0.64 us (2%)
    pallas_call x1, Pallas kernels, shards(): pl.pallas_call(functools.partial(kernel, n, haps, inside), out_shape=outs...  36.1 us
    pallas_call x1, Pallas kernels, shards(): pl.pallas_call(finish, out_shape=finals, in_specs=[hbm] * 3, out_specs=[h...  1.89 us

profile of v8, /device:TPU:0, one launch (start us, length us, event | category | flops | bytes accessed | tf_op | source)
XLA Modules:
  0.0 38.6 jit_solution(10213236027326787152)
XLA Ops:
  0.6 36.1 %shard_map.93 = (bf16[128,512]{1,0:T(8,128)(2,1)}, bf16[2,4,64,256]{3,2,1,0:T(8,128)(2,1)}, f32[4,8,128]{2,1,0:T(8,128)}) custom-call(bf16[128,512]{1,0:T(8,128)(2,1)} %bitcast.5, bf16[128,512]{1,0:T(8,128)(2,1)} %bitcast.6, s32[1,2]{1,0:T(1,128)} %gaps_hbm.1, f32[3,2,512]{2,1,0:T(2,128)} %bitcast.7, f32[2,512]{1,0:T(2,128)} %gains_hbm.1, ...), custom_call_target="tpu_custom_call" | custom-call | tf_op jit(solution)/shard_map/pallas_call | solution.py:548
  36.7 1.9 %shard_map.94 = (bf16[128,512]{1,0:T(8,128)(2,1)}, f32[2,64,1024]{2,1,0:T(8,128)}, f32[3,2,512]{2,1,0:T(2,128)}, f32[2,512]{1,0:T(2,128)}) custom-call(bf16[128,512]{1,0:T(8,128)(2,1)} %get-tuple-element.11.tg, bf16[2,4,64,256]{3,2,1,0:T(8,128)(2,1)} %get-tuple-element.12.pg, f32[4,8,128]{2,1,0:T(8,128)} %get-tuple-element.13.sm), custom_call_target="tpu_custom_call" | custom-call | tf_op jit(solution)/shard_map/pallas_call | solution.py:560
